TPU v7x, 128 devices: a whole 4x4x4 slice. The times are simulated.
128 devices in a mesh: grp: 8 (over x, z_hi), unit: 16 (over z_lo, y, core).
Axes of the slice: x: 4, y: 4, z: 4 (z_hi: 2, z_lo: 2; z = z_hi * 2 + z_lo), core: 2. Of those that a mesh axis runs over, the one named last changes fastest.
Arguments:
- x_fp: bfloat16 [768, 4096], P(('grp', 'unit')), may hold values from -6 to 6
- x_q: bfloat16 [768, 4096], P(('grp', 'unit')), may hold values from -6 to 6
- expert_ids: int32 [768, 8], P(('grp', 'unit')), may hold values from 0 to 15, all different within a row; in each aligned block of 6 rows (0 to 5, 6 to 11, ...) at most 4 rows name the same one
- route_weight: float32 [768, 8], P(('grp', 'unit')), may hold values from 0.05 to 0.4
- gate_weight: bfloat16 [16, 1536, 4096], P('grp', 'unit'), may hold values from -0.09375 to 0.09375
- up_weight: bfloat16 [16, 1536, 4096], P('grp', 'unit'), may hold values from -0.09375 to 0.09375
- down_weight: bfloat16 [16, 1536, 4096], P('grp', 'unit'), may hold values from -0.15625 to 0.15625
- gate_clip: float32 [2, 16, 1536], P(None, 'grp', 'unit'), may hold values from 0 to 4
- up_clip: float32 [2, 16, 1536], P(None, 'grp', 'unit'), may hold values from 0 to 4
- down_clip: float32 [2, 16, 4096], P(None, 'grp'), may hold values from 0 to 4
Outputs:
- gate_clip_grad: float32 [2, 16, 1536], P(None, 'grp', 'unit')
- up_clip_grad: float32 [2, 16, 1536], P(None, 'grp', 'unit')
- down_clip_grad: float32 [2, 16, 4096], P(None, 'grp', 'unit')
Inputs may be any that keep to these rules, and one draw needn't show every extreme that they name: `expert_ids`: in each aligned block of 6 rows (the tokens of one device) no expert is named by more than 4 rows; a row names 8 different experts.
All inputs are finite; a program needn't handle non-finite values.
Results may differ from a plain program's by a relative error of at most 0.03.
Values may be sent and summed in bfloat16 or wider, within the bound.
A program may use at most 128 MiB of HBM per device.

v0:
```python
import jax
import jax.numpy as jnp
from jax import lax
from jax.sharding import PartitionSpec as P


def ste_floor(value):
    return value + lax.stop_gradient(jnp.floor(value + 0.5) - value)


def fake_quant(weight_f, upper, lower, col_max, col_min):
    high_end = jax.nn.sigmoid(upper) * col_max
    low_end = jax.nn.sigmoid(lower) * col_min
    step_size = (high_end - low_end) / 15.0
    zero_point = ste_floor(-low_end / step_size)
    levels = jnp.clip(ste_floor(weight_f / step_size) + zero_point, 0.0, 15.0)
    return (levels - zero_point) * step_size


def on_device(
    x_fp,
    x_q,
    expert_ids,
    route_weight,
    gate_weight,
    up_weight,
    down_weight,
    gate_clip,
    up_clip,
    down_clip,
):
    groups = lax.axis_size("grp")
    tok_count, feat_width = x_fp.shape
    top_count = expert_ids.shape[1]
    exp_local = gate_weight.shape[0]
    expert_total = exp_local * groups
    capacity = (tok_count * top_count * 4 + 3 * expert_total - 1) // (3 * expert_total)
    highest = lax.Precision.HIGHEST
    flat_ids = expert_ids.reshape(-1)
    onehot = (flat_ids[:, None] == jnp.arange(expert_total, dtype=jnp.int32)[None, :]).astype(
        jnp.int32
    )
    slot_pos = jnp.sum(jnp.cumsum(onehot, axis=0) * onehot, axis=1) - 1
    row_expert = jnp.repeat(jnp.arange(expert_total, dtype=jnp.int32), capacity)
    row_slot = jnp.tile(jnp.arange(capacity, dtype=jnp.int32), expert_total)
    chooser = (
        (flat_ids[None, :] == row_expert[:, None]) & (slot_pos[None, :] == row_slot[:, None])
    ).astype(jnp.float32)
    pick_rows = jnp.sum(chooser.reshape(-1, tok_count, top_count), axis=2).astype(jnp.bfloat16)
    combine = jnp.sum(
        (chooser * route_weight.reshape(-1)[None, :]).reshape(-1, tok_count, top_count), axis=2
    )
    send_fp = (
        jnp.dot(pick_rows, x_fp, preferred_element_type=jnp.float32)
        .astype(jnp.bfloat16)
        .reshape(expert_total, capacity, feat_width)
    )
    send_q = (
        jnp.dot(pick_rows, x_q, preferred_element_type=jnp.float32)
        .astype(jnp.bfloat16)
        .reshape(expert_total, capacity, feat_width)
    )
    fp_in, q_in = (
        lax.all_to_all(send_fp, "grp", split_axis=0, concat_axis=1, tiled=True),
        lax.all_to_all(send_q, "grp", split_axis=0, concat_axis=1, tiled=True),
    )
    fp_rows, q_rows = (
        lax.all_gather(fp_in, "unit", axis=1, tiled=True),
        lax.all_gather(q_in, "unit", axis=1, tiled=True),
    )
    gate_f = gate_weight.astype(jnp.float32)
    up_f = up_weight.astype(jnp.float32)
    down_f = down_weight.astype(jnp.float32)
    down_top, down_neg = (
        lax.pmax(jnp.max(down_f, axis=1).astype(jnp.bfloat16), "unit").astype(jnp.float32),
        lax.pmax((-jnp.min(down_f, axis=1)).astype(jnp.bfloat16), "unit").astype(jnp.float32),
    )
    gate_max = jnp.max(gate_f, axis=2, keepdims=True)
    gate_min = jnp.min(gate_f, axis=2, keepdims=True)
    up_max = jnp.max(up_f, axis=2, keepdims=True)
    up_min = jnp.min(up_f, axis=2, keepdims=True)

    def quant_gate(upper, lower):
        return fake_quant(gate_f, upper[:, :, None], lower[:, :, None], gate_max, gate_min)

    def quant_up(upper, lower):
        return fake_quant(up_f, upper[:, :, None], lower[:, :, None], up_max, up_min)

    def quant_down(upper, lower):
        return fake_quant(
            down_f,
            upper[:, None, :],
            lower[:, None, :],
            down_top[:, None, :],
            -down_neg[:, None, :],
        )

    gate_q, gate_back = jax.vjp(quant_gate, gate_clip[0], gate_clip[1])
    up_q, up_back = jax.vjp(quant_up, up_clip[0], up_clip[1])
    down_q, down_back = jax.vjp(quant_down, down_clip[0], down_clip[1])
    gate_qb = gate_q.astype(jnp.bfloat16)
    up_qb = up_q.astype(jnp.bfloat16)
    down_qb = down_q.astype(jnp.bfloat16)
    teacher_gate = jnp.einsum(
        "erd,efd->erf", fp_rows, gate_weight, preferred_element_type=jnp.float32
    )
    teacher_up = jnp.einsum("erd,efd->erf", fp_rows, up_weight, preferred_element_type=jnp.float32)
    teacher_hidden = (jax.nn.silu(teacher_gate) * teacher_up).astype(jnp.bfloat16)
    student_gate = jnp.einsum("erd,efd->erf", q_rows, gate_qb, preferred_element_type=jnp.float32)
    student_up = jnp.einsum("erd,efd->erf", q_rows, up_qb, preferred_element_type=jnp.float32)
    student_hidden = (jax.nn.silu(student_gate) * student_up).astype(jnp.bfloat16)
    difference = jnp.einsum(
        "erf,efd->erd", student_hidden, down_qb, preferred_element_type=jnp.float32
    ) - jnp.einsum("erf,efd->erd", teacher_hidden, down_weight, preferred_element_type=jnp.float32)
    summed = lax.psum_scatter(
        difference.astype(jnp.bfloat16), "unit", scatter_dimension=1, tiled=True
    )
    returned = lax.all_to_all(summed, "grp", split_axis=1, concat_axis=0, tiled=True)
    token_diff = jnp.dot(
        combine.T, returned.reshape(-1, feat_width).astype(jnp.float32), precision=highest
    )
    token_cot = token_diff.astype(jnp.bfloat16)
    slot_cot = (
        jnp.dot(combine, token_cot.astype(jnp.float32), precision=highest)
        .astype(jnp.bfloat16)
        .reshape(expert_total, capacity, feat_width)
    )
    cot_in = lax.all_to_all(slot_cot, "grp", split_axis=0, concat_axis=1, tiled=True)
    cot_rows = lax.all_gather(cot_in, "unit", axis=1, tiled=True)
    d_hidden = jnp.einsum("erd,efd->erf", cot_rows, down_qb, preferred_element_type=jnp.float32)
    gate_sig = jax.nn.sigmoid(student_gate)
    d_gate = (d_hidden * student_up * gate_sig * (1.0 + student_gate * (1.0 - gate_sig))).astype(
        jnp.bfloat16
    )
    d_up = (d_hidden * student_gate * gate_sig).astype(jnp.bfloat16)
    dq_gate = jnp.einsum("erf,erd->efd", d_gate, q_rows, preferred_element_type=jnp.float32)
    dq_up = jnp.einsum("erf,erd->efd", d_up, q_rows, preferred_element_type=jnp.float32)
    dq_down = jnp.einsum(
        "erf,erd->efd", student_hidden, cot_rows, preferred_element_type=jnp.float32
    )
    gate_grad = jnp.stack(gate_back(dq_gate))
    up_grad = jnp.stack(up_back(dq_up))
    down_grad = lax.psum_scatter(
        jnp.stack(down_back(dq_down)).astype(jnp.bfloat16), "unit", scatter_dimension=2, tiled=True
    ).astype(jnp.float32)
    return (gate_grad, up_grad, down_grad)


def solution(mesh):
    in_specs = (
        P(("grp", "unit"), None),
        P(("grp", "unit"), None),
        P(("grp", "unit"), None),
        P(("grp", "unit"), None),
        P("grp", "unit", None),
        P("grp", "unit", None),
        P("grp", "unit", None),
        P(None, "grp", "unit"),
        P(None, "grp", "unit"),
        P(None, "grp", None),
    )
    out_specs = (P(None, "grp", "unit"), P(None, "grp", "unit"), P(None, "grp", "unit"))
    return jax.shard_map(
        on_device, mesh=mesh, in_specs=in_specs, out_specs=out_specs, check_vma=False
    )
```

profile of v0, /device:TPU:1, one launch (start us, length us, event | category | flops | bytes accessed | tf_op | source)
XLA Modules:
  0.0 425.2 jit_solution(4899309606873859602)
XLA Ops:
  8.6 1.4 select_reduce_fusion
  10.6 17.5 %all_to_all.69 = bf16[16,4,4096]{2,1,0:T(4,128)(2,1)S(1)} all-to-all(bf16[16,4,4096]{2,1,0:T(4,128)(2,1)S(1)} %reshape.503), channel_id=1, replica_groups=mesh['grp'=8,'unit'=16] {'grp'}, dimensions={0} | all-to-all | bytes 1048576 | tf_op jit(solution)/shard_map/all_to_all | solution.py:65
  29.9 12.3 %all_to_all.70 = bf16[16,4,4096]{2,1,0:T(4,128)(2,1)S(1)} all-to-all(bf16[16,4,4096]{2,1,0:T(4,128)(2,1)S(1)} %reshape.504), channel_id=1, replica_groups=mesh['grp'=8,'unit'=16] {'grp'}, dimensions={0} | all-to-all | bytes 1048576 | tf_op jit(solution)/shard_map/all_to_all | solution.py:64
  43.2 2.0 all_to_all.57
  45.3 1.8 reduce_max.48
  48.0 53.3 %all-reduce = (bf16[2,4096]{1,0:T(2,128)(2,1)S(1)}, bf16[2,4096]{1,0:T(2,128)(2,1)S(1)}) all-reduce(bf16[2,4096]{1,0:T(2,128)(2,1)S(1)} %reduce_max.52, bf16[2,4096]{1,0:T(2,128)(2,1)S(1)} %negate_convert_fusion), channel_id=1, replica_groups=mesh['grp'=8,'unit'=16] {'unit'}, use_global_device_ids=true, to_apply=%region_9.11 | all-reduce | flops 16384 | bytes 65536 | tf_op jit(solution)/shard_map/pmax | solution.py:75
  101.3 1.7 convert_reduce_fusion.2
  105.5 6.9 %fusion.9 = f32[2,512,96]{1,2,0:T(8,128)S(1)} fusion(bf16[2,512,4096]{2,1,0:T(8,128)(2,1)} %all-gather.4.cloned.1.call-done, f32[2,96]{1,0:T(2,128)S(1)} %subtract_add_fusion.5, f32[2,96]{1,0:T(2,128)S(1)} %get-tuple-element.49, bf16[2,96,4096]{2,1,0:T(8,128)(2,1)} %param.17), kind=kOutput, calls=%fused_computation.41 | convolution fusion | flops 813957120 | bytes 10356224 | tf_op jit(solution)/shard_map/erd,efd->erf/dot_general | solution.py:109
  112.4 3.6 multiply_convert_fusion.7
  116.1 8.3 %fusion.31 = f32[2,512,4096]{2,1,0:T(8,128)} fusion(bf16[2,512,96]{1,2,0:T(8,128)(2,1)S(1)} %get-tuple-element.50, f32[2,4096]{1,0:T(2,128)S(1)} %subtract_add_fusion.3, f32[2,4096]{1,0:T(2,128)S(1)} %get-tuple-element.40, bf16[2,96,4096]{2,1,0:T(8,128)(2,1)S(1)} %copy-done.2), kind=kOutput, calls=%fused_computation.72 | convolution fusion | flops 813957120 | bytes 18612224 | tf_op jit(solution)/shard_map/erf,efd->erd/dot_general | solution.py:112
  124.3 14.4 %all-gather.6.cloned.1.call-done = bf16[2,512,4096]{2,1,0:T(8,128)(2,1)} async-done(((bf16[2,32,4096]{2,1,0:T(8,128)(2,1)}), bf16[2,512,4096]{2,1,0:T(8,128)(2,1)}) %all-gather.6.cloned.1.call-update) | async-done | bytes 8388624 | tf_op jit(solution)/shard_map/all_gather | solution.py:68
  138.8 6.5 %fusion.78 = f32[2,512,96]{1,2,0:T(8,128)S(1)} fusion(bf16[2,512,4096]{2,1,0:T(8,128)(2,1)} %all-gather.6.cloned.1.call-done, bf16[2,96,4096]{2,1,0:T(8,128)(2,1)} %param.17), kind=kOutput, calls=%fused_computation.166 | convolution fusion | flops 805306368 | bytes 10354688 | tf_op jit(solution)/shard_map/erd,efd->erf/dot_general | solution.py:104
  145.3 15.6 %subtract_convert_fusion = bf16[2,512,4096]{2,1,0:T(8,128)(2,1)} fusion(f32[2,512,4096]{2,1,0:T(8,128)} %fusion.31, bf16[2,96,4096]{2,1,0:T(8,128)(2,1)S(1)} %copy-done.2, bf16[2,512,4096]{2,1,0:T(8,128)(2,1)} %all-gather.6.cloned.1.call-done, bf16[2,96,4096]{2,1,0:T(8,128)(2,1)S(1)} %copy-done.3, f32[2,512,96]{1,2,0:T(8,128)S(1)} %fusion.78), kind=kOutput, calls=%fused_computation | convolution fusion | flops 1619591168 | bytes 37093376 | tf_op jit(solution)/shard_map/erf,efd->erd/dot_general | solution.py:114
  161.0 71.4 %reduce-scatter.5.cloned.1.call-done = bf16[2,32,4096]{2,1,0:T(8,128)(2,1)} async-done(((bf16[2,512,4096]{2,1,0:T(8,128)(2,1)}), bf16[2,32,4096]{2,1,0:T(8,128)(2,1)}) %reduce-scatter.5.cloned.1.call-update) | async-done | bytes 524304 | tf_op jit(solution)/shard_map/reduce_scatter | solution.py:115
  232.4 1.6 copy.27
  234.0 14.6 %all_to_all.71 = bf16[2,32,4096]{2,0,1:T(2,128)(2,1)S(1)} all-to-all(bf16[2,32,4096]{2,0,1:T(2,128)(2,1)S(1)} %copy.27), channel_id=1, replica_groups=mesh['grp'=8,'unit'=16] {'grp'}, dimensions={1} | all-to-all | bytes 1048576 | tf_op jit(solution)/shard_map/all_to_all | solution.py:118
  248.6 1.2 copy.37
  249.8 1.9 reshape.505
  251.7 1.4 convolution_convert_fusion.3
  253.1 1.4 convolution_convert_fusion.2
  254.6 2.0 reshape.506
  256.6 12.1 %all_to_all.72 = bf16[16,4,4096]{2,1,0:T(4,128)(2,1)S(1)} all-to-all(bf16[16,4,4096]{2,1,0:T(4,128)(2,1)} %reshape.506), channel_id=1, replica_groups=mesh['grp'=8,'unit'=16] {'grp'}, dimensions={0} | all-to-all | bytes 1048576 | tf_op jit(solution)/shard_map/all_to_all | solution.py:128
  268.7 1.1 copy.36
  269.7 2.0 all_to_all.64
  272.1 56.4 %all-gather.8.cloned.1.call-done = bf16[2,512,4096]{2,1,0:T(8,128)(2,1)} async-done(((bf16[2,32,4096]{2,1,0:T(8,128)(2,1)}), bf16[2,512,4096]{2,1,0:T(8,128)(2,1)}) %all-gather.8.cloned.1.call-update) | async-done | bytes 8388624 | tf_op jit(solution)/shard_map/all_gather | solution.py:129
  328.6 8.0 %fusion.68 = (f32[2,4096]{1,0:T(2,128)S(1)}, f32[2,4096]{1,0:T(2,128)S(1)}, f32[2,4096]{1,0:T(2,128)S(1)}, f32[2,4096]{1,0:T(2,128)S(1)}) fusion(f32[2,4096]{1,0:T(2,128)S(1)} %copy-done.6, f32[2,4096]{1,0:T(2,128)S(1)} %copy-done.10, bf16[2,96,4096]{2,1,0:T(8,128)(2,1)S(1)} %copy-done.2, f32[2,4096]{1,0:T(2,128)S(1)} %copy-done.18, ...), kind=kOutput, calls=%fused_computation.165 | convolution fusion | flops 827293696 | bytes 10387456 | tf_op jit(solution)/shard_map/erf,erd->efd/dot_general | solution.py:138
  336.9 3.5 fusion.30
  340.5 8.3 %fusion.66 = (f32[2,96]{1,0:T(2,128)S(1)}, f32[2,96]{1,0:T(2,128)S(1)}, f32[2,96]{1,0:T(2,128)S(1)}, f32[2,96]{1,0:T(2,128)S(1)}) fusion(f32[2,96]{1,0:T(2,128)S(1)} %copy-done.34, f32[2,96]{1,0:T(2,128)S(1)} %copy-done.40, bf16[2,96,4096]{2,1,0:T(8,128)(2,1)S(1)} %copy-done.4, f32[2,96]{1,0:T(2,128)S(1)} %copy-done.38, ...), kind=kOutput, calls=%fused_computation.163 | convolution fusion | flops 828308736 | bytes 11146496 | tf_op jit(solution)/shard_map/erf,erd->efd/dot_general | solution.py:136
  349.1 4.8 %fusion.67 = (f32[2,96]{1,0:T(2,128)S(1)}, f32[2,96]{1,0:T(2,128)S(1)}, f32[2,96]{1,0:T(2,128)S(1)}, f32[2,96]{1,0:T(2,128)S(1)}) fusion(f32[2,96]{1,0:T(2,128)S(1)} %copy-done.32, f32[2,96]{1,0:T(2,128)S(1)} %copy-done.37, bf16[2,96,4096]{2,1,0:T(8,128)(2,1)S(1)} %copy-done.3, f32[2,96]{1,0:T(2,128)S(1)} %copy-done.35, ...), kind=kOutput, calls=%fused_computation.164 | convolution fusion | flops 827915520 | bytes 10753280 | tf_op jit(solution)/shard_map/erf,erd->efd/dot_general | solution.py:137
  354.0 2.8 copy.30
  356.8 1.8 reshape.509
  359.2 57.8 %reduce-scatter.7.cloned.1.call-done = bf16[256,4]{1,0:T(8,128)(2,1)} async-done(((bf16[4096,4]{1,0:T(8,128)(2,1)}), bf16[256,4]{1,0:T(8,128)(2,1)}) %reduce-scatter.7.cloned.1.call-update) | async-done | bytes 2064
  (147 shorter events, 11.1 us)
Async XLA Ops:
  7.2 22.1 %copy-start.14 = (bf16[6,4096]{1,0:T(8,128)(2,1)S(1)}, bf16[6,4096]{1,0:T(8,128)(2,1)}, u32[]{:S(2)}) copy-start(bf16[6,4096]{1,0:T(8,128)(2,1)} %param.13) | copy-start | bytes 147460
  7.2 98.2 %all-gather.4.cloned.1.call-start = ((), (), s32[]{:S(2)}) async-start(), calls=%async_computation.6 | async-start | bytes 8912896 | tf_op jit(solution)/shard_map/all_gather | solution.py:69
  29.3 109.5 %all-gather.6.cloned.1.call-start = ((), (), s32[]{:S(2)}) async-start(), calls=%async_computation.7 | async-start | bytes 8912896 | tf_op jit(solution)/shard_map/all_gather | solution.py:68
  29.7 17.4 %copy-start.3 = (bf16[2,96,4096]{2,1,0:T(8,128)(2,1)S(1)}, bf16[2,96,4096]{2,1,0:T(8,128)(2,1)}, u32[]{:S(2)}) copy-start(bf16[2,96,4096]{2,1,0:T(8,128)(2,1)} %param.18) | copy-start | bytes 4718596
  45.2 187.2 %reduce-scatter.5.cloned.1.call-start = ((), (), s32[]{:S(2)}) async-start(), calls=%async_computation.8 | async-start | bytes 8912896 | tf_op jit(solution)/shard_map/reduce_scatter | solution.py:115
  47.1 56.9 %copy-start.29 = (bf16[2,96]{1,0:T(2,128)(2,1)}, bf16[2,96]{1,0:T(2,128)(2,1)S(1)}, u32[]{:S(2)}) copy-start(bf16[2,96]{1,0:T(2,128)(2,1)S(1)} %reduce_max.48) | copy-start | bytes 1156
  47.4 55.9 %copy-start.27 = (bf16[2,96]{1,0:T(2,128)(2,1)}, bf16[2,96]{1,0:T(2,128)(2,1)S(1)}, u32[]{:S(2)}) copy-start(bf16[2,96]{1,0:T(2,128)(2,1)S(1)} %reduce_max.50) | copy-start | bytes 1156
  47.4 55.9 %copy-start.25 = (f32[2,2,96]{2,1,0:T(2,128)S(1)}, f32[2,2,96]{2,1,0:T(2,128)}, u32[]{:S(2)}) copy-start(f32[2,2,96]{2,1,0:T(2,128)} %param.21) | copy-start | bytes 4612
  47.4 56.5 %copy-start.23 = (f32[2,2,96]{2,1,0:T(2,128)S(1)}, f32[2,2,96]{2,1,0:T(2,128)}, u32[]{:S(2)}) copy-start(f32[2,2,96]{2,1,0:T(2,128)} %param.20) | copy-start | bytes 4612
  47.4 57.1 %copy-start.7 = (f32[2,2,4096]{2,1,0:T(2,128)S(1)}, f32[2,2,4096]{2,1,0:T(2,128)}, u32[]{:S(2)}) copy-start(f32[2,2,4096]{2,1,0:T(2,128)} %param.22) | copy-start | bytes 196612
  103.9 8.5 %copy-start.31 = (f32[2,96]{1,0:T(2,128)}, f32[2,96]{1,0:T(2,128)S(1)}, u32[]{:S(2)}) copy-start(f32[2,96]{1,0:T(2,128)S(1)} %get-tuple-element.45) | copy-start | bytes 2308
  103.9 8.4 %copy-start.36 = (f32[2,96]{1,0:T(2,128)}, f32[2,96]{1,0:T(2,128)S(1)}, u32[]{:S(2)}) copy-start(f32[2,96]{1,0:T(2,128)S(1)} %subtract_add_fusion.4) | copy-start | bytes 2308
  105.3 10.8 %copy-start.5 = (f32[2,4096]{1,0:T(2,128)}, f32[2,4096]{1,0:T(2,128)S(1)}, u32[]{:S(2)}) copy-start(f32[2,4096]{1,0:T(2,128)S(1)} %get-tuple-element.40) | copy-start | bytes 98308
  105.4 10.7 %copy-start.9 = (f32[2,4096]{1,0:T(2,128)}, f32[2,4096]{1,0:T(2,128)S(1)}, u32[]{:S(2)}) copy-start(f32[2,4096]{1,0:T(2,128)S(1)} %subtract_add_fusion.3) | copy-start | bytes 98308
  160.9 90.8 %copy-start.17 = (f32[64,6]{0,1:T(8,128)S(1)}, f32[64,6]{0,1:T(8,128)}, u32[]{:S(2)}) copy-start(f32[64,6]{0,1:T(8,128)} %get-tuple-element.33) | copy-start | bytes 4612
  160.9 167.6 %all-gather.8.cloned.1.call-start = ((), (), s32[]{:S(2)}) async-start(), calls=%async_computation.9 | async-start | bytes 8912896 | tf_op jit(solution)/shard_map/all_gather | solution.py:129
  251.7 76.8 %copy-start.6 = (f32[2,4096]{1,0:T(2,128)S(1)}, f32[2,4096]{1,0:T(2,128)}, u32[]{:S(2)}) copy-start(f32[2,4096]{1,0:T(2,128)} %copy-done.5) | copy-start | bytes 98308
  251.7 76.8 %copy-start.10 = (f32[2,4096]{1,0:T(2,128)S(1)}, f32[2,4096]{1,0:T(2,128)}, u32[]{:S(2)}) copy-start(f32[2,4096]{1,0:T(2,128)} %copy-done.9) | copy-start | bytes 98308
  251.7 76.8 %copy-start.12 = (bf16[2,512,96]{1,2,0:T(8,128)(2,1)S(1)}, bf16[2,512,96]{1,2,0:T(8,128)(2,1)}, u32[]{:S(2)}) copy-start(bf16[2,512,96]{1,2,0:T(8,128)(2,1)} %copy-done.11) | copy-start | bytes 589828
  251.7 76.8 %copy-start.18 = (f32[2,4096]{1,0:T(2,128)S(1)}, f32[2,4096]{1,0:T(2,128)}, u32[]{:S(2)}) copy-start(f32[2,4096]{1,0:T(2,128)} %get-tuple-element.39) | copy-start | bytes 98308
  271.7 145.3 %reduce-scatter.7.cloned.1.call-start = ((), (), s32[]{:S(2)}) async-start(), calls=%async_computation.10 | async-start | bytes 1114112
  336.9 12.0 %slice-start = ((s8[8388608]{0:T(1024)(128)(4,1)}), s8[4194304]{0:T(1024)(128)(4,1)S(1)}, s32[]{:S(2)}) async-start(s8[8388608]{0:T(1024)(128)(4,1)} %bitcast.160), calls=%async_computation.11 | async-start | bytes 8388608
  340.5 8.4 %copy-start.22 = (f32[2,96]{1,0:T(2,128)S(1)}, f32[2,96]{1,0:T(2,128)}, u32[]{:S(2)}) copy-start(f32[2,96]{1,0:T(2,128)} %copy-done.21) | copy-start | bytes 2308
  340.5 8.4 %copy-start.24 = (f32[2,2,96]{2,1,0:T(2,128)S(1)}, f32[2,2,96]{2,1,0:T(2,128)}, u32[]{:S(2)}) copy-start(f32[2,2,96]{2,1,0:T(2,128)} %param.20) | copy-start | bytes 4612
  340.5 8.4 %copy-start.30 = (bf16[2,96]{1,0:T(2,128)(2,1)S(1)}, bf16[2,96]{1,0:T(2,128)(2,1)}, u32[]{:S(2)}) copy-start(bf16[2,96]{1,0:T(2,128)(2,1)} %copy-done.29) | copy-start | bytes 1156
  340.5 8.5 %copy-start.32 = (f32[2,96]{1,0:T(2,128)S(1)}, f32[2,96]{1,0:T(2,128)}, u32[]{:S(2)}) copy-start(f32[2,96]{1,0:T(2,128)} %copy-done.31) | copy-start | bytes 2308
  340.5 8.5 %copy-start.35 = (f32[2,96]{1,0:T(2,128)S(1)}, f32[2,96]{1,0:T(2,128)}, u32[]{:S(2)}) copy-start(f32[2,96]{1,0:T(2,128)} %get-tuple-element.44) | copy-start | bytes 2308
  340.5 8.5 %copy-start.37 = (f32[2,96]{1,0:T(2,128)S(1)}, f32[2,96]{1,0:T(2,128)}, u32[]{:S(2)}) copy-start(f32[2,96]{1,0:T(2,128)} %copy-done.36) | copy-start | bytes 2308
  340.5 8.5 %slice-start.1 = ((s8[8388608]{0:T(1024)(128)(4,1)}), s8[4194304]{0:T(1024)(128)(4,1)S(1)}, s32[]{:S(2)}) async-start(s8[8388608]{0:T(1024)(128)(4,1)} %bitcast.160), calls=%async_computation.12 | async-start | bytes 8388608
  340.5 8.5 %copy-start.43 = (f32[2,512,96]{1,2,0:T(8,128)S(1)}, f32[2,512,96]{1,2,0:T(8,128)}, u32[]{:S(2)}) copy-start(f32[2,512,96]{1,2,0:T(8,128)} %fusion.30) | copy-start | bytes 1179652
  340.5 8.5 %copy-start.45 = (f32[2,512,96]{1,2,0:T(8,128)S(1)}, f32[2,512,96]{1,2,0:T(8,128)}, u32[]{:S(2)}) copy-start(f32[2,512,96]{1,2,0:T(8,128)} %copy-done.44) | copy-start | bytes 1179652
  353.9 64.7 %copy-start.1 = (bf16[6,4096]{1,0:T(8,128)(2,1)S(1)}, bf16[6,4096]{1,0:T(8,128)(2,1)}, u32[]{:S(2)}) copy-start(bf16[6,4096]{1,0:T(8,128)(2,1)} %param.14) | copy-start | bytes 147460
  (21 other events, 105.2 us)
Sparse Core Ops, SparseCore 0:
  29.4 54.5 all-gather.3
  85.7 53.0 all-gather.5
  161.0 71.3 reduce-scatter.4
  271.9 56.5 all-gather.7
  358.7 58.2 reduce-scatter.6
where the time goes:
time: 429 us; the launch traced here: 425 us
  waiting for transfers between devices  200 us (47%)
  blocking collectives  110 us (26%)
  matrix products  69.1 us (16%)
  local copies, waits for them, and re-layouts  21.1 us (5%)
  between operations  14.5 us (3%)
  other arithmetic  9.93 us (2%)
    reduce_scatter x1, waiting for transfers between devices, on_device(): lax.psum_scatter(difference.astype(jnp.bfloat16), 'unit', scatter_dimensi...  71.4 us
    unnamed x6, waiting for transfers between devices  57.9 us
    all_gather x1, waiting for transfers between devices, on_device(): cot_rows = lax.all_gather(cot_in, 'unit', axis=1, tiled=True)  56.4 us
    pmax x1, blocking collectives, on_device(): lax.pmax(jnp.max(down_f, axis=1).astype(jnp.bfloat16), 'unit')  53.3 us
    all_to_all x1, blocking collectives, on_device(): lax.all_to_all(send_q, 'grp', split_axis=0, concat_axis=1, tiled=True)  17.5 us
    dot_general x1, matrix products, on_device(): jnp.einsum('erf,efd->erd', teacher_hidden, down_weight, preferred_element...  15.6 us
    all_to_all x1, blocking collectives, on_device(): lax.all_to_all(summed, 'grp', split_axis=1, concat_axis=0, tiled=True)  14.6 us
    all_gather x1, waiting for transfers between devices, on_device(): lax.all_gather(fp_in, 'unit', axis=1, tiled=True)  14.4 us
  transfers between devices with their start and end apart: 5, of which 4 were waited for; matrix products, arithmetic and copies ran while one was open for 6% of the time, Pallas kernels for 0%

commit v1 on v0

v1 whole, which is shorter than its diff:
```python
import jax
import jax.numpy as jnp
from jax import lax
from jax.experimental import pallas as pl
from jax.experimental.pallas import tpu as pltpu
from jax.sharding import PartitionSpec as P

MESH = pl.DeviceIdType.MESH
D = 4096
BF = jnp.bfloat16
F32 = jnp.float32
ORDERS = ("xyz", "yzx", "zxy")


def place():
    g, u = lax.axis_index("grp"), lax.axis_index("unit")
    x, z = lax.div(g, 2), lax.rem(g, 2) * 2 + lax.div(u, 8)
    y, c = lax.rem(lax.div(u, 2), 4), lax.rem(u, 2)
    return dict(x=x, y=y, z=z, c=c)


def device(at):
    return (at["x"] * 2 + lax.div(at["z"], 2), lax.rem(at["z"], 2) * 8 + at["y"] * 2 + at["c"])


def moved(at, **by):
    out = dict(at)
    for axis, step in by.items():
        out[axis] = lax.rem(at[axis] + step, 2 if axis == "c" else 4)
    return out


def remote(src, dst, send, recv, to):
    return pltpu.make_async_remote_copy(
        src_ref=src, dst_ref=dst, send_sem=send, recv_sem=recv, device_id=device(to), device_id_type=MESH)


def columns(y, c, full):
    if full:
        return pl.ds(pl.multiple_of(c * 2048, 2048), 2048)
    return pl.ds(pl.multiple_of(c * 2048 + y * 512, 512), 512)


def slab(at, part, phase, pos, half, mats):
    order = ORDERS[part]
    done, axis = order[:phase], order[phase]
    where = dict(at)
    where[axis] = pos
    rows = [slice(None) if a in done else pl.ds(where[a], 1) for a in "zx"]
    full = "y" in done
    width = 2048 if full else 512
    base = where["c"] * 2048 + (0 if full else where["y"] * 512)
    if mats == 2:
        lead = pl.ds(half, 1) if half is not None else slice(None)
    else:
        lead = slice(None)
        if half is not None:
            width = width // 2
            base = base + half * width
    cols = pl.ds(pl.multiple_of(base, width), width)
    return (lead, pl.ds(part, 1), rows[0], rows[1], slice(None), cols)


def gather(at, buf, send, recv, mats, between=None):
    partner = moved(at, c=1)
    sends, lands = [], []

    def push(idx, sems, to):
        cp = remote(buf.at[idx], buf.at[idx], send.at[sems], recv.at[sems], to)
        cp.start()
        sends.append(cp)

    def landed(idx, sems, at_from):
        remote(buf.at[idx], buf.at[idx], send.at[sems], recv.at[sems], at_from).wait_recv()

    def to_partner(idx, sems):
        push(idx, sems, partner)
        lands.append((idx, sems))

    def mirrored(idx, base_c):
        return idx

    for part in range(3):
        idx = slab(at, part, 0, at[ORDERS[part][0]], None, mats)
        push(idx, (part, 0, 8), partner)
        lands.append(((part, 0, at[ORDERS[part][0]], None), (part, 0, 8)))
    for phase in range(3):
        for part in range(3):
            axis = ORDERS[part][phase]
            idx = slab(at, part, phase, at[axis], None, mats)
            push(idx, (part, phase, 0), moved(at, **{axis: 1}))
            push(idx, (part, phase, 1), moved(at, **{axis: 3}))
        if between is not None:
            between(phase)
        for part in range(3):
            axis = ORDERS[part][phase]
            for side, step in ((0, 1), (1, 3)):
                origin = lax.rem(at[axis] + 4 - step, 4)
                idx = slab(at, part, phase, origin, None, mats)
                landed(idx, (part, phase, side), moved(at, **{axis: 4 - step}))
                half = slab(at, part, phase, origin, side, mats)
                push(half, (part, phase, 2 + side), moved(at, **{axis: step}))
                push(idx, (part, phase, 4 + side), partner)
                lands.append(((part, phase, origin, None), (part, phase, 4 + side)))
        for part in range(3):
            axis = ORDERS[part][phase]
            origin = lax.rem(at[axis] + 2, 4)
            for side, step in ((0, 1), (1, 3)):
                idx = slab(at, part, phase, origin, side, mats)
                landed(idx, (part, phase, 2 + side), moved(at, **{axis: 4 - step}))
                push(idx, (part, phase, 6 + side), partner)
                lands.append(((part, phase, origin, side), (part, phase, 6 + side)))
    for (part, phase, pos, half), sems in lands:
        landed(slab(partner, part, phase, pos, half, mats), sems, partner)
    for cp in sends:
        cp.wait_send()


def peer(at, n):
    u = lax.rem(lax.rem(at["z"], 2) * 8 + at["y"] * 2 + at["c"] + n, 16)
    return dict(x=at["x"], z=lax.div(at["z"], 2) * 2 + lax.div(u, 8), y=lax.rem(lax.div(u, 2), 4), c=lax.rem(u, 2)), u


def friends(at):
    out = [peer(at, n)[0] for n in range(1, 16)] + [moved(at, x=n) for n in (1, 2, 3)]
    low = lax.rem(at["z"], 2)
    return out + [dict(at, z=lax.rem(at["z"] - low + n, 4)) for n in (2, 3)]


def greet(at, others):
    barrier = pltpu.get_barrier_semaphore()
    for to in others:
        pl.semaphore_signal(barrier, inc=1, device_id=device(to), device_id_type=MESH)
    pl.semaphore_wait(barrier, len(others))


def pack_rows(xf_ref, xq_ref, ids_ref, route_ref, rows_f, packed):
    lane = lax.broadcasted_iota(jnp.int32, (6, 128), 1)
    base = lax.broadcasted_iota(jnp.int32, (6, 128), 0) * 16
    dense = jnp.zeros((6, 128), F32)
    for k in range(8):
        dense = dense + jnp.where(lane == base + ids_ref[:, k:k + 1], route_ref[:, k:k + 1], 0.0)
    weights = jnp.sum(dense, axis=0, keepdims=True)
    rest = weights - weights.astype(BF).astype(F32)
    rows_f[0:6, :] = xf_ref[...].astype(F32)
    rows_f[8:14, :] = xq_ref[...].astype(F32)
    for n in range(8):
        rows_f[6:7, 512 * n:512 * n + 128] = weights
        rows_f[7:8, 512 * n:512 * n + 128] = rest
    packed[...] = rows_f[...].astype(BF)


def turn_start(at, packed, stage, sem_a, sem_b):
    sends = []
    mine = at["c"] * 4 + at["y"]
    for n in range(1, 8):
        to = moved(at, y=n // 2, c=n % 2)
        cp = remote(packed.at[:, columns(to["y"], to["c"], False)], stage.at[mine], sem_a.at[n], sem_b.at[n], to)
        cp.start()
        sends.append(cp)
    stage[mine] = packed[:, columns(at["y"], at["c"], False)]
    return sends


def turn_end(at, stage, spread, xb, wb, sem_a, sem_b, sends):
    for n in range(1, 8):
        back = moved(at, y=(4 - n // 2) % 4, c=n % 2)
        slot = back["c"] * 4 + back["y"]
        remote(stage.at[slot], stage.at[slot], sem_a.at[n], sem_b.at[n], back).wait_recv()
    for cp in sends:
        cp.wait_send()
    for j in range(8):
        for q in range(4):
            spread[q * 128 + 16 * j:q * 128 + 16 * j + 16, :] = stage[j, :, 128 * q:128 * q + 128].astype(F32)
    cols = columns(at["y"], at["c"], False)
    for mat in range(2):
        for part in range(3):
            rows = [
                jnp.concatenate(
                    [spread[pl.ds(q * 128 + 8 * mat + 2 * part + r, 8, stride=16), :] for q in range(4)], axis=1)
                for r in range(2)
            ]
            xb[mat, part, at["z"], at["x"], :, cols] = jnp.concatenate(rows, axis=0).astype(BF)
    split = [spread[pl.ds(6 + r, 8, stride=16), :] for r in range(2)]
    wb[at["x"], at["z"]] = jnp.concatenate(split, axis=0).astype(BF)


def route_start(at, wb, axis, send, recv):
    sends = []
    for n in range(1, 4):
        to = moved(at, **{axis: n})
        idx = (at["x"], at["z"]) if axis == "z" else (at["x"],)
        cp = remote(wb.at[idx], wb.at[idx], send.at[n], recv.at[n], to)
        cp.start()
        sends.append(cp)
    return sends


def route_end(at, wb, axis, send, recv, sends):
    for n in range(1, 4):
        back = moved(at, **{axis: 4 - n})
        idx = (at["x"], back["z"]) if axis == "z" else (back["x"],)
        remote(wb.at[idx], wb.at[idx], send.at[n], recv.at[n], back).wait_recv()
    for cp in sends:
        cp.wait_send()


def unit_cols(u):
    return pl.ds(pl.multiple_of(u * 256, 256), 256)


def stats_local(down_ref, most):
    for e in range(2):
        w = down_ref[e].astype(F32)
        most[e:e + 1, :] = jnp.max(w, axis=0, keepdims=True)
        most[2 + e:3 + e, :] = -jnp.min(w, axis=0, keepdims=True)
    most[4:8, :] = jnp.zeros((4, D), F32)


def spread_start(at, src, dst, send, recv):
    sends = []
    for n in range(1, 16):
        to, u = peer(at, n)
        cp = remote(src.at[:, unit_cols(u)], dst.at[n], send.at[n], recv.at[n], to)
        cp.start()
        sends.append(cp)
    return sends


def spread_end(at, dst, send, recv, sends):
    for n in range(1, 16):
        back, _ = peer(at, 16 - n)
        remote(dst.at[n], dst.at[n], send.at[n], recv.at[n], back).wait_recv()
    for cp in sends:
        cp.wait_send()


def stats_share(at, most, fin, inbox, send, recv):
    _, me = peer(at, 0)
    top = most[:, unit_cols(me)]
    for n in range(1, 16):
        top = jnp.maximum(top, inbox[n])
    fin[:, unit_cols(me)] = top
    sends = []
    for n in range(1, 16):
        to, _ = peer(at, n)
        cp = remote(fin.at[:, unit_cols(me)], fin.at[:, unit_cols(me)], send.at[n], recv.at[n], to)
        cp.start()
        sends.append(cp)
    return sends


def stats_end(at, fin, send, recv, sends):
    for n in range(1, 16):
        back, u = peer(at, 16 - n)
        remote(fin.at[:, unit_cols(u)], fin.at[:, unit_cols(u)], send.at[n], recv.at[n], back).wait_recv()
    for cp in sends:
        cp.wait_send()


def kernel(xf_ref, xq_ref, ids_ref, route_ref, down_ref, xb, wb, most_out, packed, stage, rows_f, spread,
           most, inbox, t_s, t_r, z_s, z_r, x_s, x_r, m_s, m_r, n_s, n_r, send, recv):
    at = place()
    pack_rows(xf_ref, xq_ref, ids_ref, route_ref, rows_f, packed)
    greet(at, friends(at))
    turned = turn_start(at, packed, stage, t_s, t_r)
    stats_local(down_ref, most)
    m_sends = spread_start(at, most, inbox, m_s, m_r)
    turn_end(at, stage, spread, xb, wb, t_s, t_r, turned)
    z_sends = route_start(at, wb, "z", z_s, z_r)
    held = {}

    def between(phase):
        if phase == 0:
            spread_end(at, inbox, m_s, m_r, m_sends)
            held["n"] = stats_share(at, most, most_out, inbox, n_s, n_r)
            route_end(at, wb, "z", z_s, z_r, z_sends)
            held["x"] = route_start(at, wb, "x", x_s, x_r)
        if phase == 1:
            stats_end(at, most_out, n_s, n_r, held["n"])
            route_end(at, wb, "x", x_s, x_r, held["x"])

    gather(at, xb, send, recv, 2, between)


SEM = pltpu.SemaphoreType.DMA
VM = pl.BlockSpec(memory_space=pltpu.VMEM)


def gather_x(x_fp, x_q, expert_ids, route_weight, down_weight):
    return pl.pallas_call(
        kernel,
        out_shape=(
            jax.ShapeDtypeStruct((2, 3, 4, 4, 16, D), BF),
            jax.ShapeDtypeStruct((4, 4, 16, 128), BF),
            jax.ShapeDtypeStruct((8, D), F32),
        ),
        in_specs=[VM] * 5,
        out_specs=(VM, VM, VM),
        scratch_shapes=[
            pltpu.VMEM((16, D), BF),
            pltpu.VMEM((8, 16, 512), BF),
            pltpu.VMEM((16, D), F32),
            pltpu.VMEM((512, 128), F32),
            pltpu.VMEM((8, D), F32),
            pltpu.VMEM((16, 8, 256), F32),
            SEM((8,)), SEM((8,)), SEM((4,)), SEM((4,)), SEM((4,)), SEM((4,)),
            SEM((16,)), SEM((16,)), SEM((16,)), SEM((16,)),
            SEM((3, 3, 9)), SEM((3, 3, 9)),
        ],
        compiler_params=pltpu.CompilerParams(collective_id=0, has_side_effects=True, vmem_limit_bytes=60 << 20),
    )(x_fp, x_q, expert_ids, route_weight, down_weight)


def reduce_shapes():
    out = {}
    for phase in (2, 1, 0):
        for part in range(3):
            done = ORDERS[part][:phase]
            out[phase, part] = (4 if "z" in done else 1, 4 if "x" in done else 1, 2048 if "y" in done else 512)
    return out


def local_slab(at, part, phase, pos, half):
    order = ORDERS[part]
    done, axis = order[:phase], order[phase]
    where = dict(at)
    where[axis] = pos
    rows = [slice(None) if a in done else pl.ds(where[a], 1) for a in "zx"]
    full = "y" in done
    width = 2048 if full else 512
    base = 0 if full else where["y"] * 512
    if half is not None:
        width = width // 2
        base = base + half * width
    return (part, rows[0], rows[1], slice(None), pl.ds(pl.multiple_of(base, width), width))


def add(dst, dst_idx, *others):
    total = dst[dst_idx].astype(F32)
    for ref, idx in others:
        total = total + ref[idx].astype(F32)
    dst[dst_idx] = total.astype(BF)


def reduce_scatter(at, acc, halves, fulls, send, recv):
    sends = []

    def push(src, dst, sems, to):
        cp = remote(src, dst, send.at[sems], recv.at[sems], to)
        cp.start()
        sends.append(cp)

    def landed(dst, sems, at_from):
        remote(dst, dst, send.at[sems], recv.at[sems], at_from).wait_recv()

    for phase in (2, 1, 0):
        for part in range(3):
            axis = ORDERS[part][phase]
            width = reduce_shapes()[phase, part][2] // 2
            opposite = lax.rem(at[axis] + 2, 4)
            hb = halves[phase][part]
            fb = fulls[phase][part]
            for side, step in ((0, 1), (1, 3)):
                to = moved(at, **{axis: step})
                push(acc.at[local_slab(at, part, phase, opposite, side)], hb.at[side], (part, phase, side), to)
                near = lax.rem(at[axis] + step, 4)
                other = 1 - side
                push(acc.at[local_slab(at, part, phase, near, other)],
                     fb.at[side, :, :, :, pl.ds(other * width, width)], (part, phase, 2 + side), to)
        for part in range(3):
            axis = ORDERS[part][phase]
            width = reduce_shapes()[phase, part][2] // 2
            hb = halves[phase][part]
            fb = fulls[phase][part]
            for side, step in ((0, 1), (1, 3)):
                back = moved(at, **{axis: 4 - step})
                to = moved(at, **{axis: step})
                landed(hb.at[side], (part, phase, side), back)
                near = lax.rem(at[axis] + step, 4)
                idx = local_slab(at, part, phase, near, side)
                add(acc, idx, (hb, side))
                push(acc.at[idx], fb.at[side, :, :, :, pl.ds(side * width, width)], (part, phase, 4 + side), to)
        for part in range(3):
            axis = ORDERS[part][phase]
            width = reduce_shapes()[phase, part][2] // 2
            fb = fulls[phase][part]
            for side, step in ((0, 1), (1, 3)):
                back = moved(at, **{axis: 4 - step})
                other = 1 - side
                landed(fb.at[side, :, :, :, pl.ds(other * width, width)], (part, phase, 2 + side), back)
                landed(fb.at[side, :, :, :, pl.ds(side * width, width)], (part, phase, 4 + side), back)
            add(acc, local_slab(at, part, phase, at[axis], None), (fb, 0), (fb, 1))
    for cp in sends:
        cp.wait_send()


def ar_kernel(diff, cot, acc, theirs, *rest):
    halves = {ph: rest[3 * n:3 * n + 3] for n, ph in enumerate((2, 1, 0))}
    fulls = {ph: rest[9 + 3 * n:12 + 3 * n] for n, ph in enumerate((2, 1, 0))}
    swap_s, swap_r, rs_s, rs_r, ag_s, ag_r = rest[18:]
    at = place()
    partner = moved(at, c=1)
    others = [partner] + [moved(at, **{a: s}) for a in "xyz" for s in (1, 3)]
    greet(at, others)
    mine = pl.ds(pl.multiple_of(at["c"] * 2048, 2048), 2048)
    yours = pl.ds(pl.multiple_of(partner["c"] * 2048, 2048), 2048)
    cps = []
    for part in range(3):
        cp = remote(diff.at[part, :, :, :, yours], theirs.at[part], swap_s.at[part], swap_r.at[part], partner)
        cp.start()
        cps.append(cp)
    for part in range(3):
        cps[part].wait_recv()

        def rows(n, carry):
            acc[part, n] = (diff[part, n, :, :, mine].astype(F32) + theirs[part, n].astype(F32)).astype(BF)
            return carry
        lax.fori_loop(0, 4, rows, 0)
    reduce_scatter(at, acc, halves, fulls, rs_s, rs_r)
    for part in range(3):
        block = acc[part, at["z"], at["x"], :, pl.ds(pl.multiple_of(at["y"] * 512, 512), 512)]
        cot[0, part, at["z"], at["x"], :, columns(at["y"], at["c"], False)] = block
    gather(at, cot, ag_s, ag_r, 1)
    for cp in cps:
        cp.wait_send()


def all_reduce(diff):
    shapes = reduce_shapes()
    bufs = [pltpu.VMEM((2, shapes[ph, p][0], shapes[ph, p][1], 16, shapes[ph, p][2] // 2), BF) for ph in (2, 1, 0) for p in range(3)]
    bufs += [pltpu.VMEM((2, shapes[ph, p][0], shapes[ph, p][1], 16, shapes[ph, p][2]), BF) for ph in (2, 1, 0) for p in range(3)]
    return pl.pallas_call(
        ar_kernel,
        out_shape=jax.ShapeDtypeStruct((1, 3, 4, 4, 16, D), BF),
        in_specs=[pl.BlockSpec(memory_space=pltpu.VMEM)],
        out_specs=pl.BlockSpec(memory_space=pltpu.VMEM),
        scratch_shapes=[pltpu.VMEM((3, 4, 4, 16, 2048), BF), pltpu.VMEM((3, 4, 4, 16, 2048), BF)] + bufs + [
            pltpu.SemaphoreType.DMA((3,)), pltpu.SemaphoreType.DMA((3,)),
            pltpu.SemaphoreType.DMA((3, 3, 6)), pltpu.SemaphoreType.DMA((3, 3, 6)),
            pltpu.SemaphoreType.DMA((3, 3, 9)), pltpu.SemaphoreType.DMA((3, 3, 9)),
        ],
        compiler_params=pltpu.CompilerParams(collective_id=1, has_side_effects=True, vmem_limit_bytes=60 << 20),
    )(diff)


HI = lax.Precision.HIGHEST


def nt(a, b, **kw):
    return lax.dot_general(a, b, (((1,), (1,)), ((), ())), preferred_element_type=F32, **kw)


def tn(a, b, **kw):
    return lax.dot_general(a, b, (((0,), (0,)), ((), ())), preferred_element_type=F32, **kw)


def route_rows(wb, w2):
    g = lax.axis_index("grp")
    both = (wb[:, :, 0:8, :].astype(F32) + wb[:, :, 8:16, :].astype(F32)).reshape(128, 128)
    row8 = lax.broadcasted_iota(jnp.int32, (8, 128), 0)
    lane8 = lax.broadcasted_iota(jnp.int32, (8, 128), 1)
    m = lax.broadcasted_iota(jnp.int32, (128, 256), 0)
    n = lax.broadcasted_iota(jnp.int32, (128, 256), 1)
    home = ((m >> 3) & 3) * 64 + (m >> 5) * 16 + (m & 7)
    for part in range(3):
        total = jnp.zeros((8, 256), F32)
        for r in range(2):
            pick = ((lane8 == (2 * part + r) * 16 + 2 * g + row8) & (row8 < 2)).astype(F32)
            chosen = nt(pick, both, precision=HI)
            move = (n == home + 8 * r).astype(F32)
            total = total + jnp.dot(chosen, move, preferred_element_type=F32, precision=HI)
        w2[0:96, 256 * part:256 * part + 256] = jnp.broadcast_to(total[0:1], (96, 256))
        w2[96:192, 256 * part:256 * part + 256] = jnp.broadcast_to(total[1:2], (96, 256))


def to_column(row):
    n = row.shape[1]
    eye = lax.broadcasted_iota(jnp.int32, (n, n), 0) == lax.broadcasted_iota(jnp.int32, (n, n), 1)
    return jnp.sum(jnp.where(eye, jnp.broadcast_to(row, (n, n)), 0.0), axis=1, keepdims=True)


def to_row(col):
    n = col.shape[0]
    eye = lax.broadcasted_iota(jnp.int32, (n, n), 0) == lax.broadcasted_iota(jnp.int32, (n, n), 1)
    return jnp.sum(jnp.where(eye, jnp.broadcast_to(col, (n, n)), 0.0), axis=0, keepdims=True)


def scales(upper, lower, top, low):
    high_end = jax.nn.sigmoid(upper) * top
    low_end = jax.nn.sigmoid(lower) * low
    step = (high_end - low_end) / 15.0
    zero = jnp.floor(-low_end / step + 0.5)
    return low_end, step, zero


def quantize(w, step, inv, zero):
    v = w * inv
    q = jnp.floor(v + 0.5)
    lev = jnp.clip(q, -zero, 15.0 - zero)
    m = jnp.clip(8.0 - jnp.abs(q + zero - 7.5), 0.0, 1.0)
    return lev * step, lev - m * v, m - 1.0


def quant_rows(w_ref, clip_ref, side, ws, keep):
    for e in range(2):
        keep[side, 0, 96 * e:96 * e + 96, :] = to_column(clip_ref[0, e:e + 1, :])
        keep[side, 1, 96 * e:96 * e + 96, :] = to_column(clip_ref[1, e:e + 1, :])

        def rows(n, carry):
            at = pl.multiple_of(n * 16, 16)
            w = w_ref[e, pl.ds(at, 16), :].astype(F32)
            here = pl.ds(pl.multiple_of(96 * e + n * 16, 16), 16)
            top = jnp.max(w, axis=1, keepdims=True)
            low = jnp.min(w, axis=1, keepdims=True)
            keep[side, 2, here, :] = top
            keep[side, 3, here, :] = low
            _, step, zero = scales(keep[side, 0, here, :], keep[side, 1, here, :], top, low)
            val, slope, zs = quantize(w, step, 1.0 / step, zero)
            for k, a in enumerate((val, slope, zs)):
                ws[pl.ds(pl.multiple_of(384 * k + 192 * side + 96 * e + n * 16, 16), 16), :] = a.astype(BF)
            return carry
        lax.fori_loop(0, 6, rows, 0)


def quant_down(w_ref, clip_ref, most, wd):
    for e in range(2):
        def cols(n, carry):
            c = pl.ds(pl.multiple_of(n * 512, 512), 512)
            _, step, zero = scales(clip_ref[0, e:e + 1, c], clip_ref[1, e:e + 1, c], most[e:e + 1, c], -most[2 + e:3 + e, c])
            inv = 1.0 / step

            def rows(k, carry):
                r = pl.ds(pl.multiple_of(k * 16, 16), 16)
                val, slope, zs = quantize(w_ref[e, r, c].astype(F32), step, inv, zero)
                for i, a in enumerate((val, slope, zs)):
                    wd[i, e, r, c] = a.astype(BF)
                return carry
            return lax.fori_loop(0, 6, rows, carry)
        lax.fori_loop(0, 8, cols, 0)


def silu(v):
    return v * jax.nn.sigmoid(v)


def tokens(xb, mat, part):
    return xb[mat, part].reshape(256, D)


def teacher(xb, part, gate_ref, up_ref, w2, hid):
    x = tokens(xb, 0, part)
    cols = pl.ds(pl.multiple_of(part * 256, 256), 256)
    g = nt(gate_ref[...].reshape(192, D), x)
    u = nt(up_ref[...].reshape(192, D), x)
    hid[192:384, cols] = (-(silu(g) * u * w2[:, cols])).astype(BF)


def student(xb, part, ws, w2, hid, sgu):
    x = tokens(xb, 1, part)
    cols = pl.ds(pl.multiple_of(part * 256, 256), 256)
    g = nt(ws[0:192, :], x)
    u = nt(ws[192:384, :], x)
    sgu[0, :, cols] = g
    sgu[1, :, cols] = u
    hid[0:192, cols] = (silu(g) * u * w2[:, cols]).astype(BF)


def difference(part, hid, wd, down_ref, diff):
    cols = pl.ds(pl.multiple_of(part * 256, 256), 256)
    h = hid[:, cols]

    def chunk(n, carry):
        c = pl.ds(pl.multiple_of(n * 1024, 1024), 1024)
        w = jnp.concatenate([wd[0, :, :, c].reshape(192, 1024), down_ref[:, :, c].reshape(192, 1024)], axis=0)
        diff[part, :, :, :, c] = tn(h, w).astype(BF).reshape(4, 4, 16, 1024)
        return carry
    lax.fori_loop(0, 4, chunk, 0)


def factors(xb, part, ws, w2, sgu, fac):
    x = tokens(xb, 1, part)
    cols = pl.ds(pl.multiple_of(part * 256, 256), 256)
    g, u = sgu[0, :, cols], sgu[1, :, cols]
    s = jax.nn.sigmoid(g)
    cg = w2[:, cols] * u * s * (1.0 + g * (1.0 - s))
    cu = w2[:, cols] * g * s
    for k in range(2):
        fac[k, :, cols] = cg * nt(ws[384 + 384 * k:576 + 384 * k, :], x)
        fac[2 + k, :, cols] = cu * nt(ws[576 + 384 * k:768 + 384 * k, :], x)


def each_part(fn):
    def body(part, carry):
        fn(part)
        return carry
    lax.fori_loop(0, 3, body, 0)


def back_sums(cot, part, wd, fac, sums):
    y = cot[0, part].reshape(256, D)
    cols = pl.ds(pl.multiple_of(part * 256, 256), 256)
    dh = nt(wd[0].reshape(192, D), y)
    for k in range(4):
        sums[k] = sums[k] + jnp.sum(fac[k, :, cols] * dh, axis=1, keepdims=True)


def slopes(s1, s2, upper, lower, top, low):
    low_end, step, _ = scales(upper, lower, top, low)
    d_step = s1 + s2 * low_end / step
    d_high = d_step / 15.0
    d_low = -s2 - d_high
    su, sl = jax.nn.sigmoid(upper), jax.nn.sigmoid(lower)
    return d_high * top * su * (1.0 - su), d_low * low * sl * (1.0 - sl)


def row_grads(side, sums, keep, out):
    du, dl = slopes(sums[2 * side], sums[2 * side + 1], *[keep[side, n] for n in range(4)])
    for e in range(2):
        out[0, e:e + 1, :] = to_row(du[96 * e:96 * e + 96, :])
        out[1, e:e + 1, :] = to_row(dl[96 * e:96 * e + 96, :])


def down_sums(cot, hid, wd, clip_ref, most, part_grad):
    def cols(n, carry):
        c = pl.ds(pl.multiple_of(n * 512, 512), 512)
        dq = jnp.zeros((192, 512), F32)
        for part in range(3):
            dq = dq + jnp.dot(hid[0:192, 256 * part:256 * part + 256], cot[0, part, :, :, :, c].reshape(256, 512), preferred_element_type=F32)
        for e in range(2):
            d = dq[96 * e:96 * e + 96]
            s1 = jnp.sum(d * wd[1, e, :, c].astype(F32), axis=0, keepdims=True)
            s2 = jnp.sum(d * wd[2, e, :, c].astype(F32), axis=0, keepdims=True)
            du, dl = slopes(s1, s2, clip_ref[0, e:e + 1, c], clip_ref[1, e:e + 1, c], most[e:e + 1, c], -most[2 + e:3 + e, c])
            part_grad[e:e + 1, c] = du
            part_grad[2 + e:3 + e, c] = dl
        return carry
    lax.fori_loop(0, 8, cols, 0)


def fwd_kernel(xb, wb, most, gate_ref, up_ref, down_ref, gc, uc, dc, diff, wd, fac, hid_o, keep_o, ws, hid, sgu, w2, keep):
    route_rows(wb, w2)
    quant_rows(gate_ref, gc, 0, ws, keep)
    quant_rows(up_ref, uc, 1, ws, keep)
    quant_down(down_ref, dc, most, wd)
    each_part(lambda p: teacher(xb, p, gate_ref, up_ref, w2, hid))
    each_part(lambda p: student(xb, p, ws, w2, hid, sgu))
    each_part(lambda p: difference(p, hid, wd, down_ref, diff))
    each_part(lambda p: factors(xb, p, ws, w2, sgu, fac))
    hid_o[...] = hid[0:192, :]
    keep_o[...] = keep[...]


def bwd_kernel(cot, wd, fac, hid, keep, most, dc, g_out, u_out, d_out, sums, grad, inbox, send, recv):
    at = place()
    greet(at, [peer(at, n)[0] for n in range(1, 16)])
    down_sums(cot, hid, wd, dc, most, grad)
    grad[4:8, :] = jnp.zeros((4, D), F32)
    sends = spread_start(at, grad, inbox, send, recv)
    sums[...] = jnp.zeros_like(sums)
    each_part(lambda p: back_sums(cot, p, wd, fac, sums))
    row_grads(0, sums, keep, g_out)
    row_grads(1, sums, keep, u_out)
    spread_end(at, inbox, send, recv, sends)
    _, me = peer(at, 0)
    total = grad[:, unit_cols(me)]
    for n in range(1, 16):
        total = total + inbox[n]
    for k in range(2):
        d_out[k] = total[2 * k:2 * k + 2]


def sds(shape, dt):
    return jax.ShapeDtypeStruct(shape, dt)


def on_device(x_fp, x_q, expert_ids, route_weight, gate_weight, up_weight, down_weight, gate_clip, up_clip, down_clip):
    xb, wb, most = gather_x(x_fp, x_q, expert_ids, route_weight, down_weight)
    diff, wd, fac, hid, keep = pl.pallas_call(
        fwd_kernel,
        out_shape=(sds((3, 4, 4, 16, D), BF), sds((3, 2, 96, D), BF), sds((4, 192, 768), F32), sds((192, 768), BF), sds((2, 4, 192, 1), F32)),
        in_specs=[VM] * 9,
        out_specs=(VM,) * 5,
        scratch_shapes=[pltpu.VMEM((1152, D), BF), pltpu.VMEM((384, 768), BF), pltpu.VMEM((2, 192, 768), F32),
                        pltpu.VMEM((192, 768), F32), pltpu.VMEM((2, 4, 192, 1), F32)],
        compiler_params=pltpu.CompilerParams(vmem_limit_bytes=60 << 20),
    )(xb, wb, most, gate_weight, up_weight, down_weight, gate_clip, up_clip, down_clip)
    cot = all_reduce(diff)
    return pl.pallas_call(
        bwd_kernel,
        out_shape=(sds((2, 2, 96), F32), sds((2, 2, 96), F32), sds((2, 2, 256), F32)),
        in_specs=[VM] * 7,
        out_specs=(VM,) * 3,
        scratch_shapes=[pltpu.VMEM((4, 192, 1), F32), pltpu.VMEM((8, D), F32), pltpu.VMEM((16, 8, 256), F32), SEM((16,)), SEM((16,))],
        compiler_params=pltpu.CompilerParams(collective_id=2, has_side_effects=True, vmem_limit_bytes=60 << 20),
    )(cot, wd, fac, hid, keep, most, down_clip)


def solution(mesh):
    token = P(("grp", "unit"), None)
    weight = P("grp", "unit", None)
    clip = P(None, "grp", "unit")
    return jax.shard_map(
        on_device,
        mesh=mesh,
        in_specs=(token,) * 4 + (weight,) * 3 + (clip, clip, P(None, "grp", None)),
        out_specs=(clip,) * 3,
        check_vma=False,
    )
```

time: 429 us -> 193 us (0.45)
  waiting for transfers between devices: 200 us -> 0 us
  Pallas kernels: 0 us -> 188 us
  blocking collectives: 110 us -> 0 us
  matrix products: 69.1 us -> 0 us
  local copies, waits for them, and re-layouts: 21.1 us -> 3.78 us
  between operations: 14.5 us -> 0.66 us
  other arithmetic: 9.93 us -> 0 us
    pallas_call x0 -> x4, Pallas kernels: none -> 188 us  [the longest x1 67.5 us: all_reduce(): pl.pallas_call(ar_kernel, out_shape=jax.ShapeDtypeStruct((1, 3, 4, 4, 16,...]
    reduce_scatter x1 -> x0, waiting for transfers between devices: 71.4 us -> none  [on_device(): lax.psum_scatter(difference.astype(jnp.bfloat16), 'unit', scatter_dimensi...]
    all_gather x3 -> x0, waiting for transfers between devices: 70.9 us -> none  [the longest x1 56.4 us: on_device(): cot_rows = lax.all_gather(cot_in, 'unit', axis=1, tiled=True)]
    dot_general x13 -> x0, matrix products: 69.1 us -> none  [the longest x1 15.6 us: on_device(): jnp.einsum('erf,efd->erd', teacher_hidden, down_weight, preferred_element...]
    unnamed x6 -> x0, waiting for transfers between devices: 57.9 us -> none
    all_to_all x4 -> x0, blocking collectives: 56.5 us -> none  [the longest x1 17.5 us: on_device(): lax.all_to_all(send_q, 'grp', split_axis=0, concat_axis=1, tiled=True)]
    pmax x1 -> x0, blocking collectives: 53.3 us -> none  [on_device(): lax.pmax(jnp.max(down_f, axis=1).astype(jnp.bfloat16), 'unit')]
    all_to_all x7 -> x0, local copies, waits for them, and re-layouts: 8.36 us -> none  [the longest x2 3.04 us: on_device(): lax.all_to_all(slot_cot, 'grp', split_axis=0, concat_axis=1, tiled=True)]
  transfers between devices with their start and end apart: 5 -> 0, of which waited for: 4 -> 0; matrix products, arithmetic and copies ran while one was open for 6% -> 0% of each run, Pallas kernels for 0% -> 0%
where the time goes in v1:
time: 193 us
  Pallas kernels  188 us (97%)
  local copies, waits for them, and re-layouts  3.78 us (2%)
    pallas_call x1, Pallas kernels, all_reduce(): pl.pallas_call(ar_kernel, out_shape=jax.ShapeDtypeStruct((1, 3, 4, 4, 16,...  67.5 us
    pallas_call x1, Pallas kernels, gather_x(): pl.pallas_call(kernel, out_shape=(jax.ShapeDtypeStruct((2, 3, 4, 4, 16, D...  59.1 us
    pallas_call x1, Pallas kernels, on_device(): pl.pallas_call(fwd_kernel, out_shape=(sds((3, 4, 4, 16, D), BF), sds((3,...  45.5 us
    pallas_call x1, Pallas kernels, on_device(): pl.pallas_call(bwd_kernel, out_shape=(sds((2, 2, 96), F32), sds((2, 2, 96...  16 us

profile of v1, /device:TPU:1, one launch (start us, length us, event | category | flops | bytes accessed | tf_op | source)
XLA Modules:
  0.0 192.6 jit_solution(13180487839050379224)
XLA Ops:
  0.6 59.1 %shard_map.121 = (bf16[2,3,4,4,16,4096]{5,4,3,2,1,0:T(8,128)(2,1)}, bf16[4,4,16,128]{3,2,1,0:T(8,128)(2,1)}, f32[8,4096]{1,0:T(8,128)}) custom-call(bf16[6,4096]{1,0:T(8,128)(2,1)} %xf_ref.1, bf16[6,4096]{1,0:T(8,128)(2,1)} %xq_ref.1, s32[6,8]{1,0:T(8,128)} %ids_ref.1, f32[6,8]{1,0:T(8,128)} %route_ref.1, bf16[2,96,4096]{2,1,0:T(8,128)(2,1)} %down_ref.3), custom_call_target="tpu_custom_call" | custom-call | tf_op jit(solution)/shard_map/pallas_call | solution.py:291
  59.8 45.5 %shard_map.122 = (bf16[3,4,4,16,4096]{4,3,2,1,0:T(8,128)(2,1)}, bf16[3,2,96,4096]{3,2,1,0:T(8,128)(2,1)}, f32[4,192,768]{2,1,0:T(8,128)}, bf16[192,768]{1,0:T(8,128)(2,1)}, f32[2,4,192,1]{3,2,1,0:T(8,128)}) custom-call(bf16[2,3,4,4,16,4096]{5,4,3,2,1,0:T(8,128)(2,1)} %get-tuple-element.11.xb, bf16[4,4,16,128]{3,2,1,0:T(8,128)(2,1)} %get-tuple-element.12.wb, ...), custom_call_target="tpu_custom_call" | custom-call | tf_op jit(solution)/shard_map/pallas_call | solution.py:679
  105.2 67.5 %shard_map.123.cot = bf16[1,3,4,4,16,4096]{5,4,3,2,1,0:T(8,128)(2,1)} custom-call(bf16[3,4,4,16,4096]{4,3,2,1,0:T(8,128)(2,1)} %get-tuple-element.14.diff), custom_call_target="tpu_custom_call" | custom-call | tf_op jit(solution)/shard_map/pallas_call | solution.py:433
  172.8 16.0 %shard_map.124 = (f32[2,2,96]{2,1,0:T(2,128)}, f32[2,2,96]{2,1,0:T(2,128)}, f32[2,2,256]{2,1,0:T(2,128)}) custom-call(bf16[1,3,4,4,16,4096]{5,4,3,2,1,0:T(8,128)(2,1)} %shard_map.123.cot, bf16[3,2,96,4096]{3,2,1,0:T(8,128)(2,1)} %get-tuple-element.15.wd, f32[4,192,768]{2,1,0:T(8,128)} %get-tuple-element.16.fac, bf16[192,768]{1,0:T(8,128)(2,1)} %get-tuple-element.17.hid, ...), custom_call_target="tpu_custom_call" | custom-call | tf_op jit(solution)/shard_map/pallas_call | solution.py:689
  188.8 1.3 copy.16
  190.0 1.3 copy.17
  191.3 1.3 copy.18

commit v2 on v1

v2 whole, which is shorter than its diff:
```python
import jax
import jax.numpy as jnp
from jax import lax
from jax.experimental import pallas as pl
from jax.experimental.pallas import tpu as pltpu
from jax.sharding import PartitionSpec as P

MESH = pl.DeviceIdType.MESH
D = 4096
BF = jnp.bfloat16
F32 = jnp.float32
ORDERS = ("xyz", "yzx", "zxy")


def place():
    g, u = lax.axis_index("grp"), lax.axis_index("unit")
    x, z = lax.div(g, 2), lax.rem(g, 2) * 2 + lax.div(u, 8)
    y, c = lax.rem(lax.div(u, 2), 4), lax.rem(u, 2)
    return dict(x=x, y=y, z=z, c=c)


def device(at):
    return (at["x"] * 2 + lax.div(at["z"], 2), lax.rem(at["z"], 2) * 8 + at["y"] * 2 + at["c"])


def moved(at, **by):
    out = dict(at)
    for axis, step in by.items():
        out[axis] = lax.rem(at[axis] + step, 2 if axis == "c" else 4)
    return out


def remote(src, dst, send, recv, to):
    return pltpu.make_async_remote_copy(
        src_ref=src, dst_ref=dst, send_sem=send, recv_sem=recv, device_id=device(to), device_id_type=MESH)


def columns(y, c, full):
    if full:
        return pl.ds(pl.multiple_of(c * 2048, 2048), 2048)
    return pl.ds(pl.multiple_of(c * 2048 + y * 512, 512), 512)


def block_index(at, part, phase, pos):
    order = ORDERS[part]
    done = order[:phase]
    where = dict(at)
    if phase < 3:
        where[order[phase]] = pos
    rows = [slice(None) if a in done else pl.ds(where[a], 1) for a in "zx"]
    if "y" in done:
        return rows, where["c"] * 2048, 2048
    return rows, where["c"] * 2048 + where["y"] * 512, 512


def slab(at, mat, part, phase, pos, half=None):
    rows, base, width = block_index(at, part, phase, pos)
    if half is not None:
        width = width // 2
        base = base + half * width
    return (mat, part, rows[0], rows[1], slice(None), pl.ds(pl.multiple_of(base, width), width))


class Gather:
    def __init__(self, at, buf, mat, part, send, recv, pending):
        self.at, self.buf, self.mat, self.part = at, buf, mat, part
        self.send, self.recv, self.pending = send, recv, pending
        self.partner = moved(at, c=1)

    def push(self, idx, sem, to):
        ref = self.buf.at[idx]
        cp = remote(ref, ref, self.send.at[sem], self.recv.at[sem], to)
        cp.start()
        self.pending.append(cp)

    def landed(self, idx, sem, back):
        ref = self.buf.at[idx]
        remote(ref, ref, self.send.at[sem], self.recv.at[sem], back).wait_recv()

    def idx(self, phase, ahead, half=None, at=None):
        at = at or self.at
        pos = None
        if phase < 3:
            pos = lax.rem(at[ORDERS[self.part][phase]] + ahead, 4)
        return slab(at, self.mat, self.part, phase, pos, half)

    def ring(self, phase, n):
        return moved(self.at, **{ORDERS[self.part][phase]: n})

    def spread(self, phase):
        for n in (1, 3, 2):
            self.push(self.idx(phase, 0), 3 * phase + n - 1, self.ring(phase, n))

    def spread_wait(self, phase):
        for n in (1, 3, 2):
            self.landed(self.idx(phase, 4 - n), 3 * phase + n - 1, self.ring(phase, 4 - n))

    def last(self):
        for side, step in ((0, 1), (1, 3)):
            self.push(self.idx(2, 0, side), 6 + side, self.ring(2, step))
        for side, step in ((0, 1), (1, 3)):
            self.push(self.idx(2, 0, 1 - side), 8 + side, self.ring(2, step))
        self.push(self.idx(2, 0), 12, self.partner)

    def last_mid(self):
        for side, step in ((0, 1), (1, 3)):
            idx = self.idx(2, 4 - step, side)
            self.landed(idx, 6 + side, self.ring(2, 4 - step))
            self.push(idx, 10 + side, self.ring(2, step))

    def last_near(self):
        for side, step in ((0, 1), (1, 3)):
            self.landed(self.idx(2, 4 - step, 1 - side), 8 + side, self.ring(2, 4 - step))
            self.push(self.idx(2, 4 - step), 13 + side, self.partner)

    def last_far(self):
        for side, step in ((0, 1), (1, 3)):
            idx = self.idx(2, 2, side)
            self.landed(idx, 10 + side, self.ring(2, 4 - step))
            self.push(idx, 15 + side, self.partner)

    def finish(self):
        self.landed(self.idx(2, 0, at=self.partner), 12, self.partner)
        for side, step in ((0, 1), (1, 3)):
            self.landed(self.idx(2, 4 - step, at=self.partner), 13 + side, self.partner)
        for side in (0, 1):
            self.landed(self.idx(2, 2, side, at=self.partner), 15 + side, self.partner)


def phase_shape(part, phase):
    done = ORDERS[part][:phase]
    return (4 if "z" in done else 1, 4 if "x" in done else 1, 16, 2048 if "y" in done else 512)


class Reduce:
    def __init__(self, at, part, acc, out, theirs, halves, fulls, b_in, c_in, buf, send, recv, pending):
        self.at, self.part, self.acc, self.out, self.theirs = at, part, acc, out, theirs
        self.halves, self.fulls, self.b_in, self.c_in, self.buf = halves, fulls, b_in, c_in, buf
        self.send, self.recv, self.pending = send, recv, pending
        self.partner = moved(at, c=1)

    def push(self, src, dst, sem, to):
        cp = remote(src, dst, self.send.at[sem], self.recv.at[sem], to)
        cp.start()
        self.pending.append(cp)

    def landed(self, dst, sem, back):
        remote(dst, dst, self.send.at[sem], self.recv.at[sem], back).wait_recv()

    def idx(self, phase, ahead, half=None):
        rows, _, width = block_index(self.at, self.part, phase, 0)
        order = ORDERS[self.part]
        where = dict(self.at)
        where[order[phase]] = lax.rem(self.at[order[phase]] + ahead, 4)
        rows = [slice(None) if a in order[:phase] else pl.ds(where[a], 1) for a in "zx"]
        base = 0 if width == 2048 else where["y"] * 512
        if half is not None:
            width = width // 2
            base = base + half * width
        return (self.part, rows[0], rows[1], slice(None), pl.ds(pl.multiple_of(base, width), width))

    def ring(self, phase, n):
        return moved(self.at, **{ORDERS[self.part][phase]: n})

    def add(self, idx, *others):
        total = self.acc[idx].astype(F32)
        for v in others:
            total = total + v.astype(F32)
        return total

    def swap(self):
        self.push(self.out.at[self.part], self.theirs.at[self.part], 0, self.partner)

    def swap_sum(self):
        self.landed(self.theirs.at[self.part], 0, self.partner)

        def rows(n, carry):
            self.acc[self.part, n] = self.add((self.part, n), self.theirs[self.part, n]).astype(BF)
            return carry
        lax.fori_loop(0, 4, rows, 0)

    def first(self):
        half = phase_shape(self.part, 2)[3] // 2
        for side, step in ((0, 1), (1, 3)):
            self.push(self.acc.at[self.idx(2, 2, side)], self.halves.at[side], 1 + side, self.ring(2, step))
        for side, step in ((0, 1), (1, 3)):
            other = 1 - side
            self.push(self.acc.at[self.idx(2, step, other)], self.fulls.at[side, :, :, :, pl.ds(other * half, half)],
                      3 + side, self.ring(2, step))

    def first_mid(self):
        half = phase_shape(self.part, 2)[3] // 2
        for side, step in ((0, 1), (1, 3)):
            self.landed(self.halves.at[side], 1 + side, self.ring(2, 4 - step))
            idx = self.idx(2, step, side)
            self.acc[idx] = self.add(idx, self.halves[side]).astype(BF)
            self.push(self.acc.at[idx], self.fulls.at[side, :, :, :, pl.ds(side * half, half)], 5 + side, self.ring(2, step))

    def first_end(self):
        half = phase_shape(self.part, 2)[3] // 2
        for side, step in ((0, 1), (1, 3)):
            for which, sem in ((1 - side, 3 + side), (side, 5 + side)):
                self.landed(self.fulls.at[side, :, :, :, pl.ds(which * half, half)], sem, self.ring(2, 4 - step))
        idx = self.idx(2, 0)
        self.acc[idx] = self.add(idx, self.fulls[0], self.fulls[1]).astype(BF)
        for n in (1, 3, 2):
            self.push(self.acc.at[self.idx(1, n)], self.b_in.at[n - 1], 6 + n, self.ring(1, n))

    def second_end(self):
        for n in (1, 3, 2):
            self.landed(self.b_in.at[n - 1], 6 + n, self.ring(1, 4 - n))
        idx = self.idx(1, 0)
        self.acc[idx] = self.add(idx, *[self.b_in[n] for n in range(3)]).astype(BF)
        for n in (1, 3, 2):
            self.push(self.acc.at[idx], self.c_in.at[n - 1], 9 + n, self.ring(0, n))

    def third_end(self):
        for n in (1, 3, 2):
            self.landed(self.c_in.at[n - 1], 9 + n, self.ring(0, 4 - n))
        total = self.add(self.idx(1, 0), *[self.c_in[n] for n in range(3)])
        pos = self.at[ORDERS[self.part][1]]
        self.buf[slab(self.at, 0, self.part, 1, pos)] = total.astype(BF)


def peer(at, n):
    u = lax.rem(lax.rem(at["z"], 2) * 8 + at["y"] * 2 + at["c"] + n, 16)
    return dict(x=at["x"], z=lax.div(at["z"], 2) * 2 + lax.div(u, 8), y=lax.rem(lax.div(u, 2), 4), c=lax.rem(u, 2)), u


def friends(at):
    out = [peer(at, n)[0] for n in range(1, 16)] + [moved(at, x=n) for n in (1, 2, 3)]
    low = lax.rem(at["z"], 2)
    return out + [dict(at, z=lax.rem(at["z"] - low + n, 4)) for n in (2, 3)]


def greet_signal(others):
    barrier = pltpu.get_barrier_semaphore()
    for to in others:
        pl.semaphore_signal(barrier, inc=1, device_id=device(to), device_id_type=MESH)


def greet_wait(others):
    pl.semaphore_wait(pltpu.get_barrier_semaphore(), len(others))


def pack_rows(xf_ref, xq_ref, ids_ref, route_ref, rows_f, packed):
    lane = lax.broadcasted_iota(jnp.int32, (6, 128), 1)
    base = lax.broadcasted_iota(jnp.int32, (6, 128), 0) * 16
    dense = jnp.zeros((6, 128), F32)
    for k in range(8):
        dense = dense + jnp.where(lane == base + ids_ref[:, k:k + 1], route_ref[:, k:k + 1], 0.0)
    weights = jnp.sum(dense, axis=0, keepdims=True)
    rest = weights - weights.astype(BF).astype(F32)
    rows_f[0:6, :] = xf_ref[...].astype(F32)
    rows_f[8:14, :] = xq_ref[...].astype(F32)
    for n in range(8):
        rows_f[6:7, 512 * n:512 * n + 128] = weights
        rows_f[7:8, 512 * n:512 * n + 128] = rest
    packed[...] = rows_f[...].astype(BF)


def turn_start(at, packed, stage, sem_a, sem_b):
    sends = []
    mine = at["c"] * 4 + at["y"]
    for n in range(1, 8):
        to = moved(at, y=n // 2, c=n % 2)
        cp = remote(packed.at[:, columns(to["y"], to["c"], False)], stage.at[mine], sem_a.at[n], sem_b.at[n], to)
        cp.start()
        sends.append(cp)
    stage[mine] = packed[:, columns(at["y"], at["c"], False)]
    return sends


def turn_end(at, stage, spread, xb, wb, sem_a, sem_b, sends):
    for n in range(1, 8):
        back = moved(at, y=(4 - n // 2) % 4, c=n % 2)
        slot = back["c"] * 4 + back["y"]
        remote(stage.at[slot], stage.at[slot], sem_a.at[n], sem_b.at[n], back).wait_recv()
    for cp in sends:
        cp.wait_send()
    for j in range(8):
        for q in range(4):
            spread[q * 128 + 16 * j:q * 128 + 16 * j + 16, :] = stage[j, :, 128 * q:128 * q + 128].astype(F32)
    cols = columns(at["y"], at["c"], False)
    for mat in range(2):
        for part in range(3):
            rows = [
                jnp.concatenate(
                    [spread[pl.ds(q * 128 + 8 * mat + 2 * part + r, 8, stride=16), :] for q in range(4)], axis=1)
                for r in range(2)
            ]
            xb[mat, part, at["z"], at["x"], :, cols] = jnp.concatenate(rows, axis=0).astype(BF)
    split = [spread[pl.ds(6 + r, 8, stride=16), :] for r in range(2)]
    wb[at["x"], at["z"]] = jnp.concatenate(split, axis=0).astype(BF)


def route_start(at, wb, axis, send, recv):
    sends = []
    for n in range(1, 4):
        to = moved(at, **{axis: n})
        idx = (at["x"], at["z"]) if axis == "z" else (at["x"],)
        cp = remote(wb.at[idx], wb.at[idx], send.at[n], recv.at[n], to)
        cp.start()
        sends.append(cp)
    return sends


def route_end(at, wb, axis, send, recv, sends):
    for n in range(1, 4):
        back = moved(at, **{axis: 4 - n})
        idx = (at["x"], back["z"]) if axis == "z" else (back["x"],)
        remote(wb.at[idx], wb.at[idx], send.at[n], recv.at[n], back).wait_recv()
    for cp in sends:
        cp.wait_send()


def unit_cols(u):
    return pl.ds(pl.multiple_of(u * 256, 256), 256)


def stats_local(down_ref, most):
    for e in range(2):
        w = down_ref[e].astype(F32)
        most[e:e + 1, :] = jnp.max(w, axis=0, keepdims=True)
        most[2 + e:3 + e, :] = -jnp.min(w, axis=0, keepdims=True)
    most[4:8, :] = jnp.zeros((4, D), F32)


def spread_start(at, src, dst, send, recv):
    sends = []
    for n in range(1, 16):
        to, u = peer(at, n)
        cp = remote(src.at[:, unit_cols(u)], dst.at[n], send.at[n], recv.at[n], to)
        cp.start()
        sends.append(cp)
    return sends


def spread_end(at, dst, send, recv, sends):
    for n in range(1, 16):
        back, _ = peer(at, 16 - n)
        remote(dst.at[n], dst.at[n], send.at[n], recv.at[n], back).wait_recv()
    for cp in sends:
        cp.wait_send()


def stats_share(at, most, fin, inbox, send, recv):
    _, me = peer(at, 0)
    top = most[:, unit_cols(me)]
    for n in range(1, 16):
        top = jnp.maximum(top, inbox[n])
    fin[:, unit_cols(me)] = top
    sends = []
    for n in range(1, 16):
        to, _ = peer(at, n)
        cp = remote(fin.at[:, unit_cols(me)], fin.at[:, unit_cols(me)], send.at[n], recv.at[n], to)
        cp.start()
        sends.append(cp)
    return sends


def stats_end(at, fin, send, recv, sends):
    for n in range(1, 16):
        back, u = peer(at, 16 - n)
        remote(fin.at[:, unit_cols(u)], fin.at[:, unit_cols(u)], send.at[n], recv.at[n], back).wait_recv()
    for cp in sends:
        cp.wait_send()


HI = lax.Precision.HIGHEST


def nt(a, b, **kw):
    return lax.dot_general(a, b, (((1,), (1,)), ((), ())), preferred_element_type=F32, **kw)


def tn(a, b, **kw):
    return lax.dot_general(a, b, (((0,), (0,)), ((), ())), preferred_element_type=F32, **kw)


def route_rows(wb, w2):
    g = lax.axis_index("grp")
    both = (wb[:, :, 0:8, :].astype(F32) + wb[:, :, 8:16, :].astype(F32)).reshape(128, 128)
    row8 = lax.broadcasted_iota(jnp.int32, (8, 128), 0)
    lane8 = lax.broadcasted_iota(jnp.int32, (8, 128), 1)
    m = lax.broadcasted_iota(jnp.int32, (128, 256), 0)
    n = lax.broadcasted_iota(jnp.int32, (128, 256), 1)
    home = ((m >> 3) & 3) * 64 + (m >> 5) * 16 + (m & 7)
    for part in range(3):
        total = jnp.zeros((8, 256), F32)
        for r in range(2):
            pick = ((lane8 == (2 * part + r) * 16 + 2 * g + row8) & (row8 < 2)).astype(F32)
            chosen = nt(pick, both, precision=HI)
            move = (n == home + 8 * r).astype(F32)
            total = total + jnp.dot(chosen, move, preferred_element_type=F32, precision=HI)
        w2[0:96, 256 * part:256 * part + 256] = jnp.broadcast_to(total[0:1], (96, 256))
        w2[96:192, 256 * part:256 * part + 256] = jnp.broadcast_to(total[1:2], (96, 256))


def to_column(row):
    n = row.shape[1]
    eye = lax.broadcasted_iota(jnp.int32, (n, n), 0) == lax.broadcasted_iota(jnp.int32, (n, n), 1)
    return jnp.sum(jnp.where(eye, jnp.broadcast_to(row, (n, n)), 0.0), axis=1, keepdims=True)


def to_row(col):
    n = col.shape[0]
    eye = lax.broadcasted_iota(jnp.int32, (n, n), 0) == lax.broadcasted_iota(jnp.int32, (n, n), 1)
    return jnp.sum(jnp.where(eye, jnp.broadcast_to(col, (n, n)), 0.0), axis=0, keepdims=True)


def scales(upper, lower, top, low):
    high_end = jax.nn.sigmoid(upper) * top
    low_end = jax.nn.sigmoid(lower) * low
    step = (high_end - low_end) / 15.0
    zero = jnp.floor(-low_end / step + 0.5)
    return low_end, step, zero


def quantize(w, step, inv, zero):
    v = w * inv
    q = jnp.floor(v + 0.5)
    lev = jnp.clip(q, -zero, 15.0 - zero)
    m = jnp.clip(8.0 - jnp.abs(q + zero - 7.5), 0.0, 1.0)
    return lev * step, lev - m * v, m - 1.0


def quant_rows(w_ref, clip_ref, side, ws, keep):
    for e in range(2):
        keep[side, 0, 96 * e:96 * e + 96, :] = to_column(clip_ref[0, e:e + 1, :])
        keep[side, 1, 96 * e:96 * e + 96, :] = to_column(clip_ref[1, e:e + 1, :])

    def rows(n, carry):
        here = pl.ds(pl.multiple_of(n * 16, 16), 16)
        line = pl.ds(pl.multiple_of(192 * side + n * 16, 16), 16)
        w = w_ref[line, :].astype(F32)
        top = jnp.max(w, axis=1, keepdims=True)
        low = jnp.min(w, axis=1, keepdims=True)
        keep[side, 2, here, :] = top
        keep[side, 3, here, :] = low
        _, step, zero = scales(keep[side, 0, here, :], keep[side, 1, here, :], top, low)
        inv = 1.0 / step

        def cols(k, carry):
            c = pl.ds(pl.multiple_of(k * 512, 512), 512)
            made = quantize(w_ref[line, c].astype(F32), step, inv, zero)
            for i, a in enumerate(made):
                ws[pl.ds(pl.multiple_of(384 * i + 192 * side + n * 16, 16), 16), c] = a.astype(BF)
            return carry
        return lax.fori_loop(0, 8, cols, carry)
    lax.fori_loop(0, 12, rows, 0)


def quant_down(w_ref, clip_ref, most, wd):
    for e in range(2):
        def cols(n, carry):
            c = pl.ds(pl.multiple_of(n * 512, 512), 512)
            _, step, zero = scales(clip_ref[0, e:e + 1, c], clip_ref[1, e:e + 1, c], most[e:e + 1, c], -most[2 + e:3 + e, c])
            inv = 1.0 / step

            def rows(k, carry):
                r = pl.ds(pl.multiple_of(k * 16, 16), 16)
                val, slope, zs = quantize(w_ref[e, r, c].astype(F32), step, inv, zero)
                for i, a in enumerate((val, slope, zs)):
                    wd[i, e, r, c] = a.astype(BF)
                return carry
            return lax.fori_loop(0, 6, rows, carry)
        lax.fori_loop(0, 8, cols, 0)


def silu(v):
    return v * jax.nn.sigmoid(v)


def tokens(xb, mat, part):
    return xb[mat, part].reshape(256, D)


def part_cols(part):
    return pl.ds(256 * part, 256)


def teacher(xb, part, w_ref, w2, hid):
    cols = part_cols(part)
    gu = nt(w_ref[...], tokens(xb, 0, part))
    hid[192:384, cols] = (-(silu(gu[0:192]) * gu[192:384] * w2[:, cols])).astype(BF)


def student(xb, part, ws, w2, hid, sgu):
    cols = part_cols(part)
    gu = nt(ws[0:384, :], tokens(xb, 1, part))
    sgu[:, cols] = gu
    hid[0:192, cols] = (silu(gu[0:192]) * gu[192:384] * w2[:, cols]).astype(BF)


def difference(at, part, hid, wd, down_ref, acc, out):
    h = hid[:, part_cols(part)]

    def chunk(n, carry):
        for dst, core in ((out, 1 - at["c"]), (acc, at["c"])):
            c = pl.ds(pl.multiple_of(core * 2048 + n * 1024, 1024), 1024)
            w = jnp.concatenate([wd[0, :, :, c].reshape(192, 1024), down_ref[:, :, c].reshape(192, 1024)], axis=0)
            dst[part, :, :, :, pl.ds(pl.multiple_of(n * 1024, 1024), 1024)] = tn(h, w).astype(BF).reshape(4, 4, 16, 1024)
        return carry
    lax.fori_loop(0, 2, chunk, 0)


def factors(xb, part, ws, w2, sgu, fac):
    cols = part_cols(part)
    a = nt(ws[384:1152, :], tokens(xb, 1, part))
    g, u = sgu[0:192, cols], sgu[192:384, cols]
    s = jax.nn.sigmoid(g)
    cg = w2[:, cols] * u * s * (1.0 + g * (1.0 - s))
    cu = w2[:, cols] * g * s
    for k in range(2):
        fac[k, :, cols] = cg * a[384 * k:384 * k + 192]
        fac[2 + k, :, cols] = cu * a[384 * k + 192:384 * k + 384]


def back_sums(xb, part, wd, fac, sums):
    cols = part_cols(part)
    dh = nt(wd[0].reshape(192, D), tokens(xb, 0, part))
    for k in range(4):
        sums[k] = sums[k] + jnp.sum(fac[k, :, cols] * dh, axis=1, keepdims=True)


def slopes(s1, s2, upper, lower, top, low):
    low_end, step, _ = scales(upper, lower, top, low)
    d_step = s1 + s2 * low_end / step
    d_high = d_step / 15.0
    d_low = -s2 - d_high
    su, sl = jax.nn.sigmoid(upper), jax.nn.sigmoid(lower)
    return d_high * top * su * (1.0 - su), d_low * low * sl * (1.0 - sl)


def row_grads(side, sums, keep, out):
    du, dl = slopes(sums[2 * side], sums[2 * side + 1], *[keep[side, n] for n in range(4)])
    for e in range(2):
        out[0, e:e + 1, :] = to_row(du[96 * e:96 * e + 96, :])
        out[1, e:e + 1, :] = to_row(dl[96 * e:96 * e + 96, :])


def down_add(xb, part, hid, dq):
    h = hid[0:192, part_cols(part)]

    def cols(n, carry):
        c = pl.ds(pl.multiple_of(n * 1024, 1024), 1024)
        new = jnp.dot(h, xb[0, part, :, :, :, c].reshape(256, 1024), preferred_element_type=F32)
        dq[:, c] = new if part == 0 else dq[:, c] + new
        return carry
    lax.fori_loop(0, 4, cols, 0)


def down_sums(xb, part, hid, dq, wd, clip_ref, most, grad):
    h = hid[0:192, part_cols(part)]

    def cols(n, carry):
        c = pl.ds(pl.multiple_of(n * 512, 512), 512)
        new = jnp.dot(h, xb[0, part, :, :, :, c].reshape(256, 512), preferred_element_type=F32)
        full = dq[:, c] + new
        for e in range(2):
            d = full[96 * e:96 * e + 96]
            s1 = jnp.sum(d * wd[1, e, :, c].astype(F32), axis=0, keepdims=True)
            s2 = jnp.sum(d * wd[2, e, :, c].astype(F32), axis=0, keepdims=True)
            du, dl = slopes(s1, s2, clip_ref[0, e:e + 1, c], clip_ref[1, e:e + 1, c], most[e:e + 1, c], -most[2 + e:3 + e, c])
            grad[e:e + 1, c] = du
            grad[2 + e:3 + e, c] = dl
        return carry
    lax.fori_loop(0, 8, cols, 0)


def kernel(xf_ref, xq_ref, ids_ref, route_ref, gate_hbm, up_hbm, down_hbm, gc, uc, dc, g_out, u_out, d_out,
           xb, wb, packed, stage, rows_f, spread, raw, down, most, fin, inbox, grad, d_inbox, ws, wd, hid, sgu, w2, keep,
           fac, dq, sums, acc, out, theirs, *rest):
    halves, fulls, b_in, c_in = (rest[3 * k:3 * k + 3] for k in range(4))
    (l_s, t_s, t_r, z_s, z_r, x_s, x_r, m_s, m_r, n_s, n_r, d_s, d_r, ag_s, ag_r, rs_s, rs_r) = rest[12:]
    at = place()
    loads = [pltpu.make_async_copy(down_hbm, down, l_s.at[0])]
    for side, src in enumerate((gate_hbm, up_hbm)):
        for e in range(2):
            lines = pl.ds(192 * side + 96 * e, 96)
            loads.append(pltpu.make_async_copy(src.at[e], raw.at[lines], l_s.at[1 + 2 * side + e]))
    for cp in loads:
        cp.start()
    others = friends(at)
    greet_signal(others)
    pack_rows(xf_ref, xq_ref, ids_ref, route_ref, rows_f, packed)
    loads[0].wait()
    stats_local(down, most)
    greet_wait(others)
    turned = turn_start(at, packed, stage, t_s, t_r)
    m_sends = spread_start(at, most, inbox, m_s, m_r)
    for cp in loads[1:3]:
        cp.wait()
    turn_end(at, stage, spread, xb, wb, t_s, t_r, turned)
    pending = []
    streams = [[Gather(at, xb, mat, p, ag_s.at[s, p], ag_r.at[s, p], pending) for p in range(3)]
               for s, mat in enumerate((0, 1, 0))]
    fp, q, ct = streams

    def each(stream, step, *args):
        for g in stream:
            getattr(g, step)(*args)

    each(fp, "spread", 0)
    each(q, "spread", 0)
    z_sends = route_start(at, wb, "z", z_s, z_r)
    quant_rows(raw, gc, 0, ws, keep)
    spread_end(at, inbox, m_s, m_r, m_sends)
    n_sends = stats_share(at, most, fin, inbox, n_s, n_r)
    each(fp, "spread_wait", 0)
    each(fp, "spread", 1)
    each(q, "spread_wait", 0)
    each(q, "spread", 1)
    route_end(at, wb, "z", z_s, z_r, z_sends)
    x_sends = route_start(at, wb, "x", x_s, x_r)
    for cp in loads[3:5]:
        cp.wait()
    quant_rows(raw, uc, 1, ws, keep)
    each(fp, "spread_wait", 1)
    each(fp, "last")
    each(q, "spread_wait", 1)
    route_end(at, wb, "x", x_s, x_r, x_sends)
    route_rows(wb, w2)
    each(fp, "last_mid")
    each(q, "last")
    stats_end(at, fin, n_s, n_r, n_sends)
    quant_down(down, dc, fin, wd)
    each(fp, "last_near")
    each(fp, "last_far")
    each(fp, "finish")
    teacher(xb, 0, raw, w2, hid)
    each(q, "last_mid")
    teacher(xb, 1, raw, w2, hid)
    teacher(xb, 2, raw, w2, hid)
    each(q, "last_near")
    each(q, "last_far")
    each(q, "finish")
    for cp in pending:
        cp.wait_send()
    del pending[:]
    red = [Reduce(at, p, acc, out, theirs, halves[p], fulls[p], b_in[p], c_in[p], xb, rs_s.at[p], rs_r.at[p], pending)
           for p in range(3)]

    def forward(p):
        student(xb, p, ws, w2, hid, sgu)
        difference(at, p, hid, wd, down, acc, out)
        red[p].swap()

    forward(0)
    forward(1)
    red[0].swap_sum()
    red[0].first()
    forward(2)
    red[1].swap_sum()
    red[1].first()
    red[0].first_mid()
    red[2].swap_sum()
    red[2].first()
    factors(xb, 0, ws, w2, sgu, fac)
    red[0].first_end()
    red[1].first_mid()
    red[2].first_mid()
    factors(xb, 1, ws, w2, sgu, fac)
    red[0].second_end()
    red[1].first_end()
    red[2].first_end()
    factors(xb, 2, ws, w2, sgu, fac)
    sums[...] = jnp.zeros_like(sums)
    grad[4:8, :] = jnp.zeros((4, D), F32)
    for p in range(3):
        red[p].third_end() if p == 0 else red[p].second_end()
        if p == 0:
            ct[0].spread(1)
    for p in (1, 2):
        red[p].third_end()
        ct[p].spread(1)
    for p in range(3):
        ct[p].spread_wait(1)
        ct[p].last()
    each(ct, "last_mid")
    for p in range(3):
        ct[p].last_near()
    for p in range(3):
        ct[p].last_far()
    for p in range(3):
        ct[p].finish()
        if p < 2:
            down_add(xb, p, hid, dq)
            back_sums(xb, p, wd, fac, sums)
    down_sums(xb, 2, hid, dq, wd, dc, fin, grad)
    d_sends = spread_start(at, grad, d_inbox, d_s, d_r)
    back_sums(xb, 2, wd, fac, sums)
    row_grads(0, sums, keep, g_out)
    row_grads(1, sums, keep, u_out)
    for cp in pending:
        cp.wait_send()
    spread_end(at, d_inbox, d_s, d_r, d_sends)
    _, me = peer(at, 0)
    total = grad[:, unit_cols(me)]
    for n in range(1, 16):
        total = total + d_inbox[n]
    for k in range(2):
        d_out[k] = total[2 * k:2 * k + 2]


SEM = pltpu.SemaphoreType.DMA
VM = pl.BlockSpec(memory_space=pltpu.VMEM)
ANY = pl.BlockSpec(memory_space=pl.ANY)


def sds(shape, dt):
    return jax.ShapeDtypeStruct(shape, dt)


def hand_over(a, b, c, x, y, z):
    x[...] = a[...]
    y[...] = b[...]
    z[...] = c[...]


def on_device(x_fp, x_q, expert_ids, route_weight, gate_weight, up_weight, down_weight, gate_clip, up_clip, down_clip):
    shapes = [phase_shape(p, 2) for p in range(3)]
    small = [phase_shape(p, 1) for p in range(3)]
    scratch = [((2, 3, 4, 4, 16, D), BF), ((4, 4, 16, 128), BF), ((16, D), BF), ((8, 16, 512), BF), ((16, D), F32),
               ((512, 128), F32), ((384, D), BF), ((2, 96, D), BF), ((8, D), F32), ((8, D), F32), ((16, 8, 256), F32),
               ((8, D), F32), ((16, 8, 256), F32), ((1152, D), BF), ((3, 2, 96, D), BF), ((384, 768), BF), ((384, 768), F32),
               ((192, 768), F32), ((2, 4, 192, 1), F32), ((4, 192, 768), F32), ((192, D), F32), ((4, 192, 1), F32),
               ((3, 4, 4, 16, 2048), BF), ((3, 4, 4, 16, 2048), BF), ((3, 4, 4, 16, 2048), BF)]
    scratch += [((2,) + s[:3] + (s[3] // 2,), BF) for s in shapes]
    scratch += [((2,) + s, BF) for s in shapes]
    scratch += [((3,) + s, BF) for s in small] * 2
    outs = (sds((2, 2, 96), F32), sds((2, 2, 96), F32), sds((2, 2, 256), F32))
    made = pl.pallas_call(
        kernel,
        out_shape=outs,
        in_specs=[VM] * 4 + [ANY] * 3 + [VM] * 3,
        out_specs=(VM,) * 3,
        scratch_shapes=[pltpu.VMEM(s, t) for s, t in scratch] + [
            SEM((5,)), SEM((8,)), SEM((8,)), SEM((4,)), SEM((4,)), SEM((4,)), SEM((4,)),
            SEM((16,)), SEM((16,)), SEM((16,)), SEM((16,)), SEM((16,)), SEM((16,)),
            SEM((3, 3, 17)), SEM((3, 3, 17)), SEM((3, 13)), SEM((3, 13))],
        compiler_params=pltpu.CompilerParams(collective_id=0, has_side_effects=True, vmem_limit_bytes=62 << 20),
    )(x_fp, x_q, expert_ids, route_weight, gate_weight, up_weight, down_weight, gate_clip, up_clip, down_clip)
    return pl.pallas_call(hand_over, out_shape=outs, in_specs=[VM] * 3, out_specs=(VM,) * 3)(*made)


def solution(mesh):
    token = P(("grp", "unit"), None)
    weight = P("grp", "unit", None)
    clip = P(None, "grp", "unit")
    return jax.shard_map(
        on_device,
        mesh=mesh,
        in_specs=(token,) * 4 + (weight,) * 3 + (clip, clip, P(None, "grp", None)),
        out_specs=(clip,) * 3,
        check_vma=False,
    )
```

time: 193 us -> 127 us (0.66)
  Pallas kernels: 188 us -> 127 us
  local copies, waits for them, and re-layouts: 3.78 us -> 0 us
    pallas_call x4 -> x2, Pallas kernels: 188 us -> 127 us  [the longest x1 125 us: on_device(): pl.pallas_call(kernel, out_shape=outs, in_specs=[VM] * 4 + [ANY] * 3 + [V...]
    unnamed x3 -> x0, local copies, waits for them, and re-layouts: 3.78 us -> none
where the time goes in v2:
time: 127 us
  Pallas kernels  127 us (100%)
    pallas_call x1, Pallas kernels, on_device(): pl.pallas_call(kernel, out_shape=outs, in_specs=[VM] * 4 + [ANY] * 3 + [V...  125 us

profile of v2, /device:TPU:1, one launch (start us, length us, event | category | flops | bytes accessed | tf_op | source)
XLA Modules:
  0.0 127.2 jit_solution(2084815293333285996)
XLA Ops:
  0.6 125.3 %shard_map.121 = (f32[2,2,96]{2,1,0:T(2,128)}, f32[2,2,96]{2,1,0:T(2,128)}, f32[2,2,256]{2,1,0:T(2,128)}) custom-call(bf16[6,4096]{1,0:T(8,128)(2,1)} %xf_ref.1, bf16[6,4096]{1,0:T(8,128)(2,1)} %xq_ref.1, s32[6,8]{1,0:T(8,128)} %ids_ref.1, f32[6,8]{1,0:T(8,128)} %route_ref.1, bf16[2,96,4096]{2,1,0:T(8,128)(2,1)} %gate_hbm.1, bf16[2,96,4096]{2,1,0:T(8,128)(2,1)} %up_hbm.1, ...), custom_call_target="tpu_custom_call" | custom-call | tf_op jit(solution)/shard_map/pallas_call | solution.py:734
  126.0 1.3 %shard_map.122 = (f32[2,2,96]{2,1,0:T(2,128)}, f32[2,2,96]{2,1,0:T(2,128)}, f32[2,2,256]{2,1,0:T(2,128)}) custom-call(f32[2,2,96]{2,1,0:T(2,128)} %get-tuple-element.6.a, f32[2,2,96]{2,1,0:T(2,128)} %get-tuple-element.7.b, f32[2,2,256]{2,1,0:T(2,128)} %get-tuple-element.8.c), custom_call_target="tpu_custom_call" | custom-call | tf_op jit(solution)/shard_map/pallas_call | solution.py:745

commit v3 on v2

v3 whole, which is shorter than its diff:
```python
import jax
import jax.numpy as jnp
from jax import lax
from jax.experimental import pallas as pl
from jax.experimental.pallas import tpu as pltpu
from jax.sharding import PartitionSpec as P

MESH = pl.DeviceIdType.MESH
D = 4096
BF = jnp.bfloat16
F32 = jnp.float32
ORDERS = ("xyz", "yzx", "zxy")
CHUNKS = 4
WIDE = 2048 // CHUNKS


def place():
    g, u = lax.axis_index("grp"), lax.axis_index("unit")
    x, z = lax.div(g, 2), lax.rem(g, 2) * 2 + lax.div(u, 8)
    y, c = lax.rem(lax.div(u, 2), 4), lax.rem(u, 2)
    return dict(x=x, y=y, z=z, c=c)


def device(at):
    return (at["x"] * 2 + lax.div(at["z"], 2), lax.rem(at["z"], 2) * 8 + at["y"] * 2 + at["c"])


def moved(at, **by):
    out = dict(at)
    for axis, step in by.items():
        out[axis] = lax.rem(at[axis] + step, 2 if axis == "c" else 4)
    return out


def remote(src, dst, send, recv, to):
    return pltpu.make_async_remote_copy(
        src_ref=src, dst_ref=dst, send_sem=send, recv_sem=recv, device_id=device(to), device_id_type=MESH)


def columns(y, c, full):
    if full:
        return pl.ds(pl.multiple_of(c * 2048, 2048), 2048)
    return pl.ds(pl.multiple_of(c * 2048 + y * 512, 512), 512)


def rows_of(at, done):
    return [slice(None) if a in done else pl.ds(at[a], 1) for a in "zx"]


def ring_pos(at, part, phase, ahead):
    axis = ORDERS[part][phase]
    return dict(at, **{axis: lax.rem(at[axis] + ahead, 4)})


def ring_step(at, part, phase, n):
    return moved(at, **{ORDERS[part][phase]: n})


class Gather:
    def __init__(self, at, buf, mat, send, recv):
        self.at, self.buf, self.mat = at, buf, mat
        self.send, self.recv = send, recv
        self.partner = moved(at, c=1)

    def block(self, part, phase, ahead, half=None, at=None):
        where = ring_pos(at or self.at, part, phase, ahead)
        done = ORDERS[part][:phase]
        width = 2048 if "y" in done else 512
        base = where["c"] * 2048 + (0 if "y" in done else where["y"] * 512)
        if half is not None:
            width = width // 2
            base = base + half * width
        rows = rows_of(where, done)
        return self.buf.at[self.mat, part, rows[0], rows[1], :, pl.ds(pl.multiple_of(base, width), width)]

    def push(self, ref, send, recv, to):
        remote(ref, ref, self.send.at[send], self.recv.at[recv], to).start()

    def landed(self, ref, recv):
        remote(ref, ref, self.send.at[0], self.recv.at[recv], self.partner).wait_recv()

    def spread(self, phase):
        for n in (2, 1, 3):
            for part in range(3):
                self.push(self.block(part, phase, 0), 0, phase, ring_step(self.at, part, phase, n))

    def spread_wait(self, phase):
        self.landed(self.buf.at[self.mat, :, 0:3, 0:1, :, 0:(512, 2048)[phase]], phase)

    def last(self):
        for swap in (0, 1):
            for part in range(3):
                for side, step in ((0, 1), (1, 3)):
                    self.push(self.block(part, 2, 0, side ^ swap), 1, 2 + swap, ring_step(self.at, part, 2, step))
        for part in range(3):
            self.push(self.block(part, 2, 0), 2, 5, self.partner)

    def last_mid(self):
        self.landed(self.buf.at[self.mat, :, 0:2, 0:1], 2)
        for part in range(3):
            for side, step in ((0, 1), (1, 3)):
                self.push(self.block(part, 2, 4 - step, side), 1, 4, ring_step(self.at, part, 2, step))

    def last_near(self):
        self.landed(self.buf.at[self.mat, :, 0:2, 0:1], 3)
        for part in range(3):
            for step in (1, 3):
                self.push(self.block(part, 2, step), 2, 5, self.partner)

    def last_far(self):
        self.landed(self.buf.at[self.mat, :, 0:2, 0:1], 4)
        for part in range(3):
            self.push(self.block(part, 2, 2), 2, 5, self.partner)

    def finish(self):
        self.landed(self.buf.at[self.mat, :, 0:2], 5)


def gathers_sent(buf, send, recv, to):
    for sem, ref in enumerate((buf.at[0, :, 0:3, 0:2, :, 0:2560], buf.at[0, :, 0:3, :], buf.at[0])):
        remote(ref, ref, send.at[sem], recv.at[0], to).wait_send()


def phase_shape(part, phase):
    done = ORDERS[part][:phase]
    return (4 if "z" in done else 1, 4 if "x" in done else 1, 16, WIDE if "y" in done else WIDE // 4)


class Reduce:
    def __init__(self, at, chunk, acc, out, theirs, a_in, b_in, c_in, buf, send, recv):
        self.at, self.chunk, self.acc, self.out, self.theirs = at, chunk, acc, out, theirs
        self.ins = {2: a_in, 1: b_in, 0: c_in}
        self.buf, self.send, self.recv = buf, send, recv
        self.partner = moved(at, c=1)

    def push(self, src, dst, send, recv, to):
        remote(src, dst, self.send.at[send], self.recv.at[self.chunk, recv], to).start()

    def landed(self, ref, recv):
        remote(ref, ref, self.send.at[0], self.recv.at[self.chunk, recv], self.partner).wait_recv()

    def own(self, part, phase, ahead):
        where = ring_pos(self.at, part, phase, ahead)
        done = ORDERS[part][:phase]
        rows = rows_of(where, done)
        width = WIDE if "y" in done else WIDE // 4
        base = 0 if "y" in done else where["y"] * width
        return (self.chunk, part, rows[0], rows[1], slice(None), pl.ds(pl.multiple_of(base, width), width))

    def whole(self, part, phase):
        done = ORDERS[part][:phase]
        rows = rows_of(self.at, done)
        width = WIDE if "y" in done else WIDE // 4
        base = self.chunk * 2 * WIDE + self.at["c"] * WIDE + (0 if "y" in done else self.at["y"] * width)
        return (0, part, rows[0], rows[1], slice(None), pl.ds(pl.multiple_of(base, width), width))

    def swap(self):
        self.push(self.out.at[self.chunk], self.theirs.at[self.chunk], 0, 0, self.partner)

    def total(self, part, phase, arrived):
        sums = self.acc[self.own(part, phase, 0)].astype(F32)
        for n in range(3):
            sums = sums + self.ins[arrived][part][self.chunk, n].astype(F32)
        return sums

    def hand_on(self, part, phase):
        for n in (2, 1, 3):
            self.push(self.acc.at[self.own(part, phase, n if phase else 0)], self.ins[phase][part].at[self.chunk, n - 1],
                      1 if phase == 2 else 2, 3 - phase, ring_step(self.at, part, phase, n))

    def first(self):
        self.landed(self.theirs.at[self.chunk], 0)

        def rows(n, carry):
            part, z = lax.div(n, 4), lax.rem(n, 4)
            mine = self.acc[self.chunk, part, z].astype(F32) + self.theirs[self.chunk, part, z].astype(F32)
            self.acc[self.chunk, part, z] = mine.astype(BF)
            return carry
        lax.fori_loop(0, 12, rows, 0)
        for part in range(3):
            self.hand_on(part, 2)

    def first_end(self):
        self.landed(self.acc.at[self.chunk, :, 0:3], 1)
        for part in range(3):
            self.acc[self.own(part, 2, 0)] = self.total(part, 2, 2).astype(BF)
            self.hand_on(part, 1)

    def second_end(self):
        self.landed(self.acc.at[self.chunk, :, 0:3, 0:1], 2)
        for part in range(3):
            self.acc[self.own(part, 1, 0)] = self.total(part, 1, 1).astype(BF)
            for n in (2, 1, 3):
                self.push(self.acc.at[self.own(part, 1, 0)], self.ins[0][part].at[self.chunk, n - 1], 2, 3,
                          ring_step(self.at, part, 0, n))

    def third_end(self):
        self.landed(self.acc.at[self.chunk, :, 0:3, 0:1], 3)
        for part in range(3):
            block = self.whole(part, 1)
            self.buf[block] = self.total(part, 1, 0).astype(BF)
            for n in (2, 1, 3):
                self.push(self.buf.at[block], self.buf.at[block], 2, 4, ring_step(self.at, part, 1, n))

    def fourth_end(self):
        self.landed(self.acc.at[self.chunk, :, 0:3, 0:1], 4)
        for n in (2, 1, 3):
            for part in range(3):
                block = self.buf.at[self.whole(part, 2)]
                self.push(block, block, 1, 5, ring_step(self.at, part, 2, n))

    def fifth_end(self):
        self.landed(self.acc.at[self.chunk, :, 0:3], 5)
        base = self.chunk * 2 * WIDE + self.at["c"] * WIDE
        block = self.buf.at[0, :, :, :, :, pl.ds(pl.multiple_of(base, WIDE), WIDE)]
        self.push(block, block, 0, 6, self.partner)

    def done(self):
        self.landed(self.acc.at[self.chunk], 6)


def reduces_sent(buf, send, recv, to):
    for sem, ref in enumerate((buf.at[0], buf.at[0, :, 0:3], buf.at[0, :, 0:3, 0:3, :, 0:2048])):
        remote(ref, ref, send.at[sem], recv.at[0, 0], to).wait_send()


def peer(at, n):
    u = lax.rem(lax.rem(at["z"], 2) * 8 + at["y"] * 2 + at["c"] + n, 16)
    return dict(x=at["x"], z=lax.div(at["z"], 2) * 2 + lax.div(u, 8), y=lax.rem(lax.div(u, 2), 4), c=lax.rem(u, 2)), u


def friends(at):
    out = [peer(at, n)[0] for n in range(1, 16)] + [moved(at, x=n) for n in (1, 2, 3)]
    low = lax.rem(at["z"], 2)
    return out + [dict(at, z=lax.rem(at["z"] - low + n, 4)) for n in (2, 3)]


def greet_signal(others):
    barrier = pltpu.get_barrier_semaphore()
    for to in others:
        pl.semaphore_signal(barrier, inc=1, device_id=device(to), device_id_type=MESH)


def greet_wait(others):
    pl.semaphore_wait(pltpu.get_barrier_semaphore(), len(others))


def pack_rows(xf_ref, xq_ref, ids_ref, route_ref, rows_f, packed):
    lane = lax.broadcasted_iota(jnp.int32, (6, 128), 1)
    base = lax.broadcasted_iota(jnp.int32, (6, 128), 0) * 16
    dense = jnp.zeros((6, 128), F32)
    for k in range(8):
        dense = dense + jnp.where(lane == base + ids_ref[:, k:k + 1], route_ref[:, k:k + 1], 0.0)
    weights = jnp.sum(dense, axis=0, keepdims=True)
    rest = weights - weights.astype(BF).astype(F32)
    rows_f[0:6, :] = xf_ref[...].astype(F32)
    rows_f[8:14, :] = xq_ref[...].astype(F32)
    for n in range(8):
        rows_f[6:7, 512 * n:512 * n + 128] = weights
        rows_f[7:8, 512 * n:512 * n + 128] = rest
    packed[...] = rows_f[...].astype(BF)


def turn_start(at, packed, stage, sems):
    mine = at["c"] * 4 + at["y"]
    for n in (4, 5, 2, 3, 6, 7, 1):
        to = moved(at, y=n // 2, c=n % 2)
        remote(packed.at[:, columns(to["y"], to["c"], False)], stage.at[mine], sems.at[0], sems.at[1], to).start()
    stage[mine] = packed[:, columns(at["y"], at["c"], False)]


def both_wait(ref, sems, to):
    cp = remote(ref, ref, sems.at[0], sems.at[1], to)
    cp.wait_recv()
    cp.wait_send()


def turn_end(at, stage, spread, xb, wb, sems):
    both_wait(stage.at[0:7], sems, moved(at, c=1))
    for j in range(8):
        for q in range(4):
            spread[q * 128 + 16 * j:q * 128 + 16 * j + 16, :] = stage[j, :, 128 * q:128 * q + 128].astype(F32)
    cols = columns(at["y"], at["c"], False)
    for mat in range(2):
        for part in range(3):
            rows = [
                jnp.concatenate(
                    [spread[pl.ds(q * 128 + 8 * mat + 2 * part + r, 8, stride=16), :] for q in range(4)], axis=1)
                for r in range(2)
            ]
            xb[mat, part, at["z"], at["x"], :, cols] = jnp.concatenate(rows, axis=0).astype(BF)
    split = [spread[pl.ds(6 + r, 8, stride=16), :] for r in range(2)]
    wb[at["x"], at["z"]] = jnp.concatenate(split, axis=0).astype(BF)


def route_start(at, wb, axis, sems):
    for n in (2, 1, 3):
        idx = (at["x"], at["z"]) if axis == "z" else (at["x"],)
        remote(wb.at[idx], wb.at[idx], sems.at[0], sems.at[1], moved(at, **{axis: n})).start()


def route_end(at, wb, axis, sems):
    both_wait(wb.at[0, 0:3] if axis == "z" else wb.at[0:3], sems, moved(at, c=1))


def unit_cols(u):
    return pl.ds(pl.multiple_of(u * 256, 256), 256)


def stats_local(down_ref, most):
    for e in range(2):
        w = down_ref[e].astype(F32)
        most[e:e + 1, :] = jnp.max(w, axis=0, keepdims=True)
        most[2 + e:3 + e, :] = -jnp.min(w, axis=0, keepdims=True)
    most[4:8, :] = jnp.zeros((4, D), F32)


def spread_start(at, src, dst, sems):
    for n in range(1, 16):
        to, u = peer(at, n)
        remote(src.at[:, unit_cols(u)], dst.at[n], sems.at[0], sems.at[1], to).start()


def spread_end(at, dst, sems):
    both_wait(dst.at[1:16], sems, moved(at, c=1))


def stats_share(at, most, fin, inbox, sems):
    _, me = peer(at, 0)
    top = most[:, unit_cols(me)]
    for n in range(1, 16):
        top = jnp.maximum(top, inbox[n])
    fin[:, unit_cols(me)] = top
    for n in range(1, 16):
        to, _ = peer(at, n)
        remote(fin.at[:, unit_cols(me)], fin.at[:, unit_cols(me)], sems.at[0], sems.at[1], to).start()


HI = lax.Precision.HIGHEST


def nt(a, b, **kw):
    return lax.dot_general(a, b, (((1,), (1,)), ((), ())), preferred_element_type=F32, **kw)


def tn(a, b, **kw):
    return lax.dot_general(a, b, (((0,), (0,)), ((), ())), preferred_element_type=F32, **kw)


def route_rows(wb, w2):
    g = lax.axis_index("grp")
    both = (wb[:, :, 0:8, :].astype(F32) + wb[:, :, 8:16, :].astype(F32)).reshape(128, 128)
    row8 = lax.broadcasted_iota(jnp.int32, (8, 128), 0)
    lane8 = lax.broadcasted_iota(jnp.int32, (8, 128), 1)
    m = lax.broadcasted_iota(jnp.int32, (128, 256), 0)
    n = lax.broadcasted_iota(jnp.int32, (128, 256), 1)
    home = ((m >> 3) & 3) * 64 + (m >> 5) * 16 + (m & 7)
    for part in range(3):
        total = jnp.zeros((8, 256), F32)
        for r in range(2):
            pick = ((lane8 == (2 * part + r) * 16 + 2 * g + row8) & (row8 < 2)).astype(F32)
            chosen = nt(pick, both, precision=HI)
            move = (n == home + 8 * r).astype(F32)
            total = total + jnp.dot(chosen, move, preferred_element_type=F32, precision=HI)
        w2[0:96, 256 * part:256 * part + 256] = jnp.broadcast_to(total[0:1], (96, 256))
        w2[96:192, 256 * part:256 * part + 256] = jnp.broadcast_to(total[1:2], (96, 256))


def to_column(row):
    n = row.shape[1]
    eye = lax.broadcasted_iota(jnp.int32, (n, n), 0) == lax.broadcasted_iota(jnp.int32, (n, n), 1)
    return jnp.sum(jnp.where(eye, jnp.broadcast_to(row, (n, n)), 0.0), axis=1, keepdims=True)


def to_row(col):
    n = col.shape[0]
    eye = lax.broadcasted_iota(jnp.int32, (n, n), 0) == lax.broadcasted_iota(jnp.int32, (n, n), 1)
    return jnp.sum(jnp.where(eye, jnp.broadcast_to(col, (n, n)), 0.0), axis=0, keepdims=True)


def scales(upper, lower, top, low):
    high_end = jax.nn.sigmoid(upper) * top
    low_end = jax.nn.sigmoid(lower) * low
    step = (high_end - low_end) / 15.0
    zero = jnp.floor(-low_end / step + 0.5)
    return low_end, step, zero


def quantize(w, step, inv, zero):
    v = w * inv
    q = jnp.floor(v + 0.5)
    lev = jnp.clip(q, -zero, 15.0 - zero)
    m = jnp.clip(8.0 - jnp.abs(q + zero - 7.5), 0.0, 1.0)
    return lev * step, lev - m * v, m - 1.0


def quant_rows(w_ref, clip_ref, side, ws, keep):
    for e in range(2):
        keep[side, 0, 96 * e:96 * e + 96, :] = to_column(clip_ref[0, e:e + 1, :])
        keep[side, 1, 96 * e:96 * e + 96, :] = to_column(clip_ref[1, e:e + 1, :])

    def rows(n, carry):
        here = pl.ds(pl.multiple_of(n * 16, 16), 16)
        line = pl.ds(pl.multiple_of(192 * side + n * 16, 16), 16)
        w = w_ref[line, :].astype(F32)
        top = jnp.max(w, axis=1, keepdims=True)
        low = jnp.min(w, axis=1, keepdims=True)
        keep[side, 2, here, :] = top
        keep[side, 3, here, :] = low
        _, step, zero = scales(keep[side, 0, here, :], keep[side, 1, here, :], top, low)
        inv = 1.0 / step

        def cols(k, carry):
            c = pl.ds(pl.multiple_of(k * 512, 512), 512)
            made = quantize(w_ref[line, c].astype(F32), step, inv, zero)
            for i, a in enumerate(made):
                ws[pl.ds(pl.multiple_of(384 * i + 192 * side + n * 16, 16), 16), c] = a.astype(BF)
            return carry
        return lax.fori_loop(0, 8, cols, carry)
    lax.fori_loop(0, 12, rows, 0)


def quant_down(w_ref, clip_ref, most, wd):
    for e in range(2):
        def cols(n, carry):
            c = pl.ds(pl.multiple_of(n * 512, 512), 512)
            _, step, zero = scales(clip_ref[0, e:e + 1, c], clip_ref[1, e:e + 1, c], most[e:e + 1, c], -most[2 + e:3 + e, c])
            inv = 1.0 / step

            def rows(k, carry):
                r = pl.ds(pl.multiple_of(k * 16, 16), 16)
                val, slope, zs = quantize(w_ref[e, r, c].astype(F32), step, inv, zero)
                for i, a in enumerate((val, slope, zs)):
                    wd[i, e, r, c] = a.astype(BF)
                return carry
            return lax.fori_loop(0, 6, rows, carry)
        lax.fori_loop(0, 8, cols, 0)


def silu(v):
    return v * jax.nn.sigmoid(v)


def tokens(xb, mat, part):
    return xb[mat, part].reshape(256, D)


def part_cols(part):
    return pl.ds(256 * part, 256)


def teacher(xb, part, w_ref, w2, hid):
    cols = part_cols(part)
    gu = nt(w_ref[...], tokens(xb, 0, part))
    hid[part, 192:384, :] = (-(silu(gu[0:192]) * gu[192:384] * w2[:, cols])).astype(BF)


def student(xb, part, ws, w2, hid, sgu):
    cols = part_cols(part)
    gu = nt(ws[0:384, :], tokens(xb, 1, part))
    sgu[:, cols] = gu
    hid[part, 0:192, :] = (silu(gu[0:192]) * gu[192:384] * w2[:, cols]).astype(BF)


def difference(at, chunk, hid, wd, down_ref, acc, out):
    for dst, core in ((out, 1 - at["c"]), (acc, at["c"])):
        c = pl.ds(pl.multiple_of(chunk * 2 * WIDE + core * WIDE, WIDE), WIDE)
        w = jnp.concatenate([wd[0, :, :, c].reshape(192, WIDE), down_ref[:, :, c].reshape(192, WIDE)], axis=0)

        def body(part, carry):
            h = hid[part]
            dst[chunk, part] = tn(h, w).astype(BF).reshape(4, 4, 16, WIDE)
            return carry
        lax.fori_loop(0, 3, body, 0)


def factors(xb, part, kind, ws, w2, sgu, fac):
    cols = part_cols(part)
    a = nt(ws[384 + 384 * kind:768 + 384 * kind, :], tokens(xb, 1, part))
    g, u = sgu[0:192, cols], sgu[192:384, cols]
    s = jax.nn.sigmoid(g)
    fac[kind, :, cols] = w2[:, cols] * u * s * (1.0 + g * (1.0 - s)) * a[0:192]
    fac[2 + kind, :, cols] = w2[:, cols] * g * s * a[192:384]


def back(chunk, xb, hid, wd, clip_ref, most, dh, grad):
    k = pl.ds(chunk * 2 * WIDE, 2 * WIDE)
    w = wd[0, :, :, k].reshape(192, 2 * WIDE)
    for part in range(3):
        new = nt(w, xb[0, part, :, :, :, k].reshape(256, 2 * WIDE))
        cols = part_cols(part)
        dh[:, cols] = new if chunk == 0 else dh[:, cols] + new

    def cols(n, carry):
        c = pl.ds(pl.multiple_of(chunk * 2 * WIDE + n * 512, 512), 512)
        dq = jnp.zeros((192, 512), F32)
        for part in range(3):
            dq = dq + jnp.dot(hid[part, 0:192, :], xb[0, part, :, :, :, c].reshape(256, 512), preferred_element_type=F32)
        for e in range(2):
            d = dq[96 * e:96 * e + 96]
            s1 = jnp.sum(d * wd[1, e, :, c].astype(F32), axis=0, keepdims=True)
            s2 = jnp.sum(d * wd[2, e, :, c].astype(F32), axis=0, keepdims=True)
            du, dl = slopes(s1, s2, clip_ref[0, e:e + 1, c], clip_ref[1, e:e + 1, c], most[e:e + 1, c], -most[2 + e:3 + e, c])
            grad[e:e + 1, c] = du
            grad[2 + e:3 + e, c] = dl
        return carry
    lax.fori_loop(0, WIDE // 256, cols, 0)


def slopes(s1, s2, upper, lower, top, low):
    low_end, step, _ = scales(upper, lower, top, low)
    d_step = s1 + s2 * low_end / step
    d_high = d_step / 15.0
    d_low = -s2 - d_high
    su, sl = jax.nn.sigmoid(upper), jax.nn.sigmoid(lower)
    return d_high * top * su * (1.0 - su), d_low * low * sl * (1.0 - sl)


def row_grads(side, fac, dh, keep, out):
    sums = [jnp.sum(fac[2 * side + k] * dh[...], axis=1, keepdims=True) for k in range(2)]
    du, dl = slopes(sums[0], sums[1], *[keep[side, n] for n in range(4)])
    for e in range(2):
        out[0, e:e + 1, :] = to_row(du[96 * e:96 * e + 96, :])
        out[1, e:e + 1, :] = to_row(dl[96 * e:96 * e + 96, :])


def kernel(xf_ref, xq_ref, ids_ref, route_ref, gate_hbm, up_hbm, down_hbm, gc, uc, dc, g_out, u_out, d_out,
           xb, wb, packed, stage, rows_f, spread, raw, down, most, fin, inbox, grad, d_inbox, ws, wd, hid, sgu, w2, keep,
           fac, dh, acc, out, theirs, *rest):
    a_in, b_in, c_in = (rest[3 * k:3 * k + 3] for k in range(3))
    l_s, t_s, z_s, x_s, m_s, n_s, d_s, ag_s, ag_r, rs_s, rs_r = rest[9:]
    at = place()
    loads = [pltpu.make_async_copy(down_hbm, down, l_s.at[0])]
    for side, src in enumerate((gate_hbm, up_hbm)):
        for e in range(2):
            lines = pl.ds(192 * side + 96 * e, 96)
            loads.append(pltpu.make_async_copy(src.at[e], raw.at[lines], l_s.at[1 + 2 * side + e]))
    others = friends(at)
    greet_signal(others)
    for cp in loads:
        cp.start()
    pack_rows(xf_ref, xq_ref, ids_ref, route_ref, rows_f, packed)
    greet_wait(others)
    turn_start(at, packed, stage, t_s)
    loads[0].wait()
    stats_local(down, most)
    spread_start(at, most, inbox, m_s)
    turn_end(at, stage, spread, xb, wb, t_s)
    fp, q = (Gather(at, xb, mat, ag_s, ag_r.at[mat]) for mat in range(2))
    fp.spread(0)
    q.spread(0)
    route_start(at, wb, "z", z_s)
    for cp in loads[1:3]:
        cp.wait()
    quant_rows(raw, gc, 0, ws, keep)
    fp.spread_wait(0)
    fp.spread(1)
    q.spread_wait(0)
    q.spread(1)
    route_end(at, wb, "z", z_s)
    route_start(at, wb, "x", x_s)
    spread_end(at, inbox, m_s)
    stats_share(at, most, fin, inbox, n_s)
    for cp in loads[3:5]:
        cp.wait()
    quant_rows(raw, uc, 1, ws, keep)
    fp.spread_wait(1)
    fp.last()
    route_end(at, wb, "x", x_s)
    route_rows(wb, w2)
    fp.last_mid()
    q.spread_wait(1)
    q.last()
    both_wait(inbox.at[1:16], n_s, moved(at, c=1))
    quant_down(down, dc, fin, wd)
    fp.last_near()
    q.last_mid()
    fp.last_far()
    fp.finish()
    for p in range(3):
        teacher(xb, p, raw, w2, hid)
    q.last_near()
    q.last_far()
    q.finish()
    gathers_sent(xb, ag_s, ag_r.at[0], moved(at, c=1))
    red = [Reduce(at, k, acc, out, theirs, a_in, b_in, c_in, xb, rs_s, rs_r) for k in range(CHUNKS)]
    for p in range(3):
        student(xb, p, ws, w2, hid, sgu)
    grad[4:8, :] = jnp.zeros((4, D), F32)
    difference(at, 0, hid, wd, down, acc, out)
    red[0].swap()
    difference(at, 1, hid, wd, down, acc, out)
    red[1].swap()
    red[0].first()
    difference(at, 2, hid, wd, down, acc, out)
    red[2].swap()
    red[1].first()
    difference(at, 3, hid, wd, down, acc, out)
    red[3].swap()
    red[2].first()
    red[3].first()
    factors(xb, 0, 0, ws, w2, sgu, fac)
    red[0].first_end()
    factors(xb, 0, 1, ws, w2, sgu, fac)
    red[1].first_end()
    red[0].second_end()
    factors(xb, 1, 0, ws, w2, sgu, fac)
    red[2].first_end()
    red[1].second_end()
    factors(xb, 1, 1, ws, w2, sgu, fac)
    red[3].first_end()
    red[0].third_end()
    red[2].second_end()
    factors(xb, 2, 0, ws, w2, sgu, fac)
    red[1].third_end()
    red[0].fourth_end()
    red[3].second_end()
    factors(xb, 2, 1, ws, w2, sgu, fac)
    red[2].third_end()
    red[1].fourth_end()
    red[0].fifth_end()
    red[3].third_end()
    red[2].fourth_end()
    red[1].fifth_end()
    red[0].done()
    back(0, xb, hid, wd, dc, fin, dh, grad)
    red[3].fourth_end()
    red[2].fifth_end()
    red[1].done()
    back(1, xb, hid, wd, dc, fin, dh, grad)
    red[3].fifth_end()
    red[2].done()
    back(2, xb, hid, wd, dc, fin, dh, grad)
    red[3].done()
    back(3, xb, hid, wd, dc, fin, dh, grad)
    spread_start(at, grad, d_inbox, d_s)
    row_grads(0, fac, dh, keep, g_out)
    row_grads(1, fac, dh, keep, u_out)
    reduces_sent(xb, rs_s, rs_r, moved(at, c=1))
    spread_end(at, d_inbox, d_s)
    _, me = peer(at, 0)
    total = grad[:, unit_cols(me)]
    for n in range(1, 16):
        total = total + d_inbox[n]
    for k in range(2):
        d_out[k] = total[2 * k:2 * k + 2]


SEM = pltpu.SemaphoreType.DMA
VM = pl.BlockSpec(memory_space=pltpu.VMEM)
ANY = pl.BlockSpec(memory_space=pl.ANY)


def sds(shape, dt):
    return jax.ShapeDtypeStruct(shape, dt)


def hand_over(a, b, c, x, y, z):
    x[...] = a[...]
    y[...] = b[...]
    z[...] = c[...]


def on_device(x_fp, x_q, expert_ids, route_weight, gate_weight, up_weight, down_weight, gate_clip, up_clip, down_clip):
    scratch = [((2, 3, 4, 4, 16, D), BF), ((4, 4, 16, 128), BF), ((16, D), BF), ((8, 16, 512), BF), ((16, D), F32),
               ((512, 128), F32), ((384, D), BF), ((2, 96, D), BF), ((8, D), F32), ((8, D), F32), ((16, 8, 256), F32),
               ((8, D), F32), ((16, 8, 256), F32), ((1152, D), BF), ((3, 2, 96, D), BF), ((3, 384, 256), BF), ((384, 768), F32),
               ((192, 768), F32), ((2, 4, 192, 1), F32), ((4, 192, 768), F32), ((192, 768), F32)]
    scratch += [((CHUNKS, 3, 4, 4, 16, WIDE), BF)] * 3
    scratch += [((CHUNKS, 3) + phase_shape(p, phase), BF) for phase in (2, 1, 1) for p in range(3)]
    outs = (sds((2, 2, 96), F32), sds((2, 2, 96), F32), sds((2, 2, 256), F32))
    made = pl.pallas_call(
        kernel,
        out_shape=outs,
        in_specs=[VM] * 4 + [ANY] * 3 + [VM] * 3,
        out_specs=(VM,) * 3,
        scratch_shapes=[pltpu.VMEM(s, t) for s, t in scratch] + [SEM((5,))] + [SEM((2,))] * 6 + [
            SEM((3,)), SEM((2, 6)), SEM((3,)), SEM((CHUNKS, 7))],
        compiler_params=pltpu.CompilerParams(collective_id=0, has_side_effects=True, vmem_limit_bytes=62 << 20),
    )(x_fp, x_q, expert_ids, route_weight, gate_weight, up_weight, down_weight, gate_clip, up_clip, down_clip)
    return pl.pallas_call(hand_over, out_shape=outs, in_specs=[VM] * 3, out_specs=(VM,) * 3)(*made)


def solution(mesh):
    token = P(("grp", "unit"), None)
    weight = P("grp", "unit", None)
    clip = P(None, "grp", "unit")
    return jax.shard_map(
        on_device,
        mesh=mesh,
        in_specs=(token,) * 4 + (weight,) * 3 + (clip, clip, P(None, "grp", None)),
        out_specs=(clip,) * 3,
        check_vma=False,
    )
```

time: 127 us -> 117 us (0.921)
  Pallas kernels: 127 us -> 116 us
    pallas_call x1, Pallas kernels: 125 us -> 115 us  [on_device(): pl.pallas_call(kernel, out_shape=outs, in_specs=[VM] * 4 + [ANY] * 3 + [V...]
where the time goes in v3:
time: 117 us
  Pallas kernels  116 us (99%)
    pallas_call x1, Pallas kernels, on_device(): pl.pallas_call(kernel, out_shape=outs, in_specs=[VM] * 4 + [ANY] * 3 + [V...  115 us

profile of v3, /device:TPU:1, one launch (start us, length us, event | category | flops | bytes accessed | tf_op | source)
XLA Modules:
  0.0 116.6 jit_solution(9624332568938489201)
XLA Ops:
  0.6 114.7 %shard_map.121 = (f32[2,2,96]{2,1,0:T(2,128)}, f32[2,2,96]{2,1,0:T(2,128)}, f32[2,2,256]{2,1,0:T(2,128)}) custom-call(bf16[6,4096]{1,0:T(8,128)(2,1)} %xf_ref.1, bf16[6,4096]{1,0:T(8,128)(2,1)} %xq_ref.1, s32[6,8]{1,0:T(8,128)} %ids_ref.1, f32[6,8]{1,0:T(8,128)} %route_ref.1, bf16[2,96,4096]{2,1,0:T(8,128)(2,1)} %gate_hbm.1, bf16[2,96,4096]{2,1,0:T(8,128)(2,1)} %up_hbm.1, ...), custom_call_target="tpu_custom_call" | custom-call | tf_op jit(solution)/shard_map/pallas_call | solution.py:672
  115.3 1.3 %shard_map.122 = (f32[2,2,96]{2,1,0:T(2,128)}, f32[2,2,96]{2,1,0:T(2,128)}, f32[2,2,256]{2,1,0:T(2,128)}) custom-call(f32[2,2,96]{2,1,0:T(2,128)} %get-tuple-element.6.a, f32[2,2,96]{2,1,0:T(2,128)} %get-tuple-element.7.b, f32[2,2,256]{2,1,0:T(2,128)} %get-tuple-element.8.c), custom_call_target="tpu_custom_call" | custom-call | tf_op jit(solution)/shard_map/pallas_call | solution.py:681

commit v4 on v3

--- a/solution.py
+++ b/solution.py
@@ -394,29 +394,36 @@
     return lev * step, lev - m * v, m - 1.0
 
 
-def quant_rows(w_ref, clip_ref, side, ws, keep):
+def quant_rows(w_ref, clip_ref, side, ws, keep, wide):
+    base = 192 * side
     for e in range(2):
         keep[side, 0, 96 * e:96 * e + 96, :] = to_column(clip_ref[0, e:e + 1, :])
         keep[side, 1, 96 * e:96 * e + 96, :] = to_column(clip_ref[1, e:e + 1, :])
+    for block in range(4):
+        lines = pl.ds(base + 48 * block, 48)
+        first = w_ref[lines, 0:128].astype(F32)
+
+        def extremes(n, carry):
+            top, low = carry
+            for k in range(4):
+                w = w_ref[lines, pl.ds(pl.multiple_of(n * 512 + 128 * k, 128), 128)].astype(F32)
+                top, low = jnp.maximum(top, w), jnp.minimum(low, w)
+            return top, low
+        top, low = lax.fori_loop(0, 8, extremes, (first, first))
+        keep[side, 2, 48 * block:48 * block + 48, :] = jnp.max(top, axis=1, keepdims=True)
+        keep[side, 3, 48 * block:48 * block + 48, :] = jnp.min(low, axis=1, keepdims=True)
+    _, step, zero = scales(*[keep[side, k] for k in range(4)])
+    for k, a in enumerate((step, 1.0 / step, zero)):
+        wide[k] = jnp.broadcast_to(a, (192, 128))
 
     def rows(n, carry):
         here = pl.ds(pl.multiple_of(n * 16, 16), 16)
-        line = pl.ds(pl.multiple_of(192 * side + n * 16, 16), 16)
-        w = w_ref[line, :].astype(F32)
-        top = jnp.max(w, axis=1, keepdims=True)
-        low = jnp.min(w, axis=1, keepdims=True)
-        keep[side, 2, here, :] = top
-        keep[side, 3, here, :] = low
-        _, step, zero = scales(keep[side, 0, here, :], keep[side, 1, here, :], top, low)
-        inv = 1.0 / step
-
-        def cols(k, carry):
-            c = pl.ds(pl.multiple_of(k * 512, 512), 512)
-            made = quantize(w_ref[line, c].astype(F32), step, inv, zero)
-            for i, a in enumerate(made):
-                ws[pl.ds(pl.multiple_of(384 * i + 192 * side + n * 16, 16), 16), c] = a.astype(BF)
-            return carry
-        return lax.fori_loop(0, 8, cols, carry)
+        step, inv, zero = (jnp.concatenate([wide[k, here, :]] * 4, axis=1) for k in range(3))
+        for c in range(8):
+            w = w_ref[pl.ds(pl.multiple_of(base + n * 16, 16), 16), 512 * c:512 * c + 512].astype(F32)
+            for i, a in enumerate(quantize(w, step, inv, zero)):
+                ws[pl.ds(pl.multiple_of(384 * i + base + n * 16, 16), 16), 512 * c:512 * c + 512] = a.astype(BF)
+        return carry
     lax.fori_loop(0, 12, rows, 0)
 
 
@@ -455,23 +462,19 @@
     hid[part, 192:384, :] = (-(silu(gu[0:192]) * gu[192:384] * w2[:, cols])).astype(BF)
 
 
-def student(xb, part, ws, w2, hid, sgu):
+def student(xb, part, ws, w2, hid, hid_t, sgu):
     cols = part_cols(part)
     gu = nt(ws[0:384, :], tokens(xb, 1, part))
     sgu[:, cols] = gu
     hid[part, 0:192, :] = (silu(gu[0:192]) * gu[192:384] * w2[:, cols]).astype(BF)
-
-
-def difference(at, chunk, hid, wd, down_ref, acc, out):
-    for dst, core in ((out, 1 - at["c"]), (acc, at["c"])):
-        c = pl.ds(pl.multiple_of(chunk * 2 * WIDE + core * WIDE, WIDE), WIDE)
-        w = jnp.concatenate([wd[0, :, :, c].reshape(192, WIDE), down_ref[:, :, c].reshape(192, WIDE)], axis=0)
-
-        def body(part, carry):
-            h = hid[part]
-            dst[chunk, part] = tn(h, w).astype(BF).reshape(4, 4, 16, WIDE)
-            return carry
-        lax.fori_loop(0, 3, body, 0)
+    hid_t[part] = jnp.transpose(hid[part].astype(F32)).astype(BF)
+
+
+def difference(chunk, core, hid_t, wd, down_ref, dst):
+    c = pl.ds(pl.multiple_of(chunk * 2 * WIDE + core * WIDE, WIDE), WIDE)
+    w = jnp.concatenate([wd[0, :, :, c].reshape(192, WIDE), down_ref[:, :, c].reshape(192, WIDE)], axis=0)
+    made = jnp.dot(hid_t[...].reshape(768, 384), w, preferred_element_type=F32)
+    dst[chunk] = made.astype(BF).reshape(3, 4, 4, 16, WIDE)
 
 
 def factors(xb, part, kind, ws, w2, sgu, fac):
@@ -525,7 +528,7 @@
 
 
 def kernel(xf_ref, xq_ref, ids_ref, route_ref, gate_hbm, up_hbm, down_hbm, gc, uc, dc, g_out, u_out, d_out,
-           xb, wb, packed, stage, rows_f, spread, raw, down, most, fin, inbox, grad, d_inbox, ws, wd, hid, sgu, w2, keep,
+           xb, wb, packed, stage, rows_f, spread, raw, down, most, fin, inbox, grad, d_inbox, ws, wd, hid, hid_t, wide, sgu, w2, keep,
            fac, dh, acc, out, theirs, *rest):
     a_in, b_in, c_in = (rest[3 * k:3 * k + 3] for k in range(3))
     l_s, t_s, z_s, x_s, m_s, n_s, d_s, ag_s, ag_r, rs_s, rs_r = rest[9:]
@@ -552,7 +555,7 @@
     route_start(at, wb, "z", z_s)
     for cp in loads[1:3]:
         cp.wait()
-    quant_rows(raw, gc, 0, ws, keep)
+    quant_rows(raw, gc, 0, ws, keep, wide)
     fp.spread_wait(0)
     fp.spread(1)
     q.spread_wait(0)
@@ -563,7 +566,7 @@
     stats_share(at, most, fin, inbox, n_s)
     for cp in loads[3:5]:
         cp.wait()
-    quant_rows(raw, uc, 1, ws, keep)
+    quant_rows(raw, uc, 1, ws, keep, wide)
     fp.spread_wait(1)
     fp.last()
     route_end(at, wb, "x", x_s)
@@ -585,18 +588,22 @@
     gathers_sent(xb, ag_s, ag_r.at[0], moved(at, c=1))
     red = [Reduce(at, k, acc, out, theirs, a_in, b_in, c_in, xb, rs_s, rs_r) for k in range(CHUNKS)]
     for p in range(3):
-        student(xb, p, ws, w2, hid, sgu)
+        student(xb, p, ws, w2, hid, hid_t, sgu)
     grad[4:8, :] = jnp.zeros((4, D), F32)
-    difference(at, 0, hid, wd, down, acc, out)
+    difference(0, 1 - at["c"], hid_t, wd, down, out)
     red[0].swap()
-    difference(at, 1, hid, wd, down, acc, out)
+    difference(0, at["c"], hid_t, wd, down, acc)
+    difference(1, 1 - at["c"], hid_t, wd, down, out)
     red[1].swap()
+    difference(1, at["c"], hid_t, wd, down, acc)
     red[0].first()
-    difference(at, 2, hid, wd, down, acc, out)
+    difference(2, 1 - at["c"], hid_t, wd, down, out)
     red[2].swap()
+    difference(2, at["c"], hid_t, wd, down, acc)
     red[1].first()
-    difference(at, 3, hid, wd, down, acc, out)
+    difference(3, 1 - at["c"], hid_t, wd, down, out)
     red[3].swap()
+    difference(3, at["c"], hid_t, wd, down, acc)
     red[2].first()
     red[3].first()
     factors(xb, 0, 0, ws, w2, sgu, fac)
@@ -664,7 +671,8 @@
 def on_device(x_fp, x_q, expert_ids, route_weight, gate_weight, up_weight, down_weight, gate_clip, up_clip, down_clip):
     scratch = [((2, 3, 4, 4, 16, D), BF), ((4, 4, 16, 128), BF), ((16, D), BF), ((8, 16, 512), BF), ((16, D), F32),
                ((512, 128), F32), ((384, D), BF), ((2, 96, D), BF), ((8, D), F32), ((8, D), F32), ((16, 8, 256), F32),
-               ((8, D), F32), ((16, 8, 256), F32), ((1152, D), BF), ((3, 2, 96, D), BF), ((3, 384, 256), BF), ((384, 768), F32),
+               ((8, D), F32), ((16, 8, 256), F32), ((1152, D), BF), ((3, 2, 96, D), BF), ((3, 384, 256), BF), ((3, 256, 384), BF), ((3, 192, 128), F32),
+               ((384, 768), F32),
                ((192, 768), F32), ((2, 4, 192, 1), F32), ((4, 192, 768), F32), ((192, 768), F32)]
     scratch += [((CHUNKS, 3, 4, 4, 16, WIDE), BF)] * 3
     scratch += [((CHUNKS, 3) + phase_shape(p, phase), BF) for phase in (2, 1, 1) for p in range(3)]

time: 117 us -> 105 us (0.90)
  Pallas kernels: 116 us -> 104 us
    pallas_call x1, Pallas kernels: 115 us -> 103 us  [on_device(): pl.pallas_call(kernel, out_shape=outs, in_specs=[VM] * 4 + [ANY] * 3 + [V...]
where the time goes in v4:
time: 105 us
  Pallas kernels  104 us (99%)
    pallas_call x1, Pallas kernels, on_device(): pl.pallas_call(kernel, out_shape=outs, in_specs=[VM] * 4 + [ANY] * 3 + [V...  103 us

profile of v4, /device:TPU:1, one launch (start us, length us, event | category | flops | bytes accessed | tf_op | source)
XLA Modules:
  0.0 104.8 jit_solution(14042447997950210902)
XLA Ops:
  0.6 102.8 %shard_map.121 = (f32[2,2,96]{2,1,0:T(2,128)}, f32[2,2,96]{2,1,0:T(2,128)}, f32[2,2,256]{2,1,0:T(2,128)}) custom-call(bf16[6,4096]{1,0:T(8,128)(2,1)} %xf_ref.1, bf16[6,4096]{1,0:T(8,128)(2,1)} %xq_ref.1, s32[6,8]{1,0:T(8,128)} %ids_ref.1, f32[6,8]{1,0:T(8,128)} %route_ref.1, bf16[2,96,4096]{2,1,0:T(8,128)(2,1)} %gate_hbm.1, bf16[2,96,4096]{2,1,0:T(8,128)(2,1)} %up_hbm.1, ...), custom_call_target="tpu_custom_call" | custom-call | tf_op jit(solution)/shard_map/pallas_call | solution.py:680
  103.5 1.3 %shard_map.122 = (f32[2,2,96]{2,1,0:T(2,128)}, f32[2,2,96]{2,1,0:T(2,128)}, f32[2,2,256]{2,1,0:T(2,128)}) custom-call(f32[2,2,96]{2,1,0:T(2,128)} %get-tuple-element.6.a, f32[2,2,96]{2,1,0:T(2,128)} %get-tuple-element.7.b, f32[2,2,256]{2,1,0:T(2,128)} %get-tuple-element.8.c), custom_call_target="tpu_custom_call" | custom-call | tf_op jit(solution)/shard_map/pallas_call | solution.py:689

commit v5 on v4

--- a/solution.py
+++ b/solution.py
@@ -462,11 +462,15 @@
     hid[part, 192:384, :] = (-(silu(gu[0:192]) * gu[192:384] * w2[:, cols])).astype(BF)
 
 
-def student(xb, part, ws, w2, hid, hid_t, sgu):
+def student_half(xb, part, core, ws, sgu, fresh):
+    k = pl.ds(pl.multiple_of(core * 2048, 2048), 2048)
+    gu = nt(ws[0:384, k], xb[1, part, :, :, :, k].reshape(256, 2048))
+    sgu[:, part_cols(part)] = gu if fresh else sgu[:, part_cols(part)] + gu
+
+
+def student(part, w2, hid, hid_t, sgu):
     cols = part_cols(part)
-    gu = nt(ws[0:384, :], tokens(xb, 1, part))
-    sgu[:, cols] = gu
-    hid[part, 0:192, :] = (silu(gu[0:192]) * gu[192:384] * w2[:, cols]).astype(BF)
+    hid[part, 0:192, :] = (silu(sgu[0:192, cols]) * sgu[192:384, cols] * w2[:, cols]).astype(BF)
     hid_t[part] = jnp.transpose(hid[part].astype(F32)).astype(BF)
 
 
@@ -486,28 +490,32 @@
     fac[2 + kind, :, cols] = w2[:, cols] * g * s * a[192:384]
 
 
-def back(chunk, xb, hid, wd, clip_ref, most, dh, grad):
-    k = pl.ds(chunk * 2 * WIDE, 2 * WIDE)
-    w = wd[0, :, :, k].reshape(192, 2 * WIDE)
+def back(at, chunk, core, xb, hid, wd, clip_ref, most, dh, grad, inbox, sems, fresh):
+    c = pl.ds(pl.multiple_of(chunk * 2 * WIDE + core * WIDE, WIDE), WIDE)
+    w = wd[0, :, :, c].reshape(192, WIDE)
+    dq = jnp.zeros((192, WIDE), F32)
     for part in range(3):
-        new = nt(w, xb[0, part, :, :, :, k].reshape(256, 2 * WIDE))
+        y = xb[0, part, :, :, :, c].reshape(256, WIDE)
+        new = nt(w, y)
         cols = part_cols(part)
-        dh[:, cols] = new if chunk == 0 else dh[:, cols] + new
-
-    def cols(n, carry):
-        c = pl.ds(pl.multiple_of(chunk * 2 * WIDE + n * 512, 512), 512)
-        dq = jnp.zeros((192, 512), F32)
-        for part in range(3):
-            dq = dq + jnp.dot(hid[part, 0:192, :], xb[0, part, :, :, :, c].reshape(256, 512), preferred_element_type=F32)
-        for e in range(2):
-            d = dq[96 * e:96 * e + 96]
-            s1 = jnp.sum(d * wd[1, e, :, c].astype(F32), axis=0, keepdims=True)
-            s2 = jnp.sum(d * wd[2, e, :, c].astype(F32), axis=0, keepdims=True)
-            du, dl = slopes(s1, s2, clip_ref[0, e:e + 1, c], clip_ref[1, e:e + 1, c], most[e:e + 1, c], -most[2 + e:3 + e, c])
-            grad[e:e + 1, c] = du
-            grad[2 + e:3 + e, c] = dl
-        return carry
-    lax.fori_loop(0, WIDE // 256, cols, 0)
+        dh[:, cols] = new if fresh else dh[:, cols] + new
+        dq = dq + jnp.dot(hid[part, 0:192, :], y, preferred_element_type=F32)
+    for e in range(2):
+        d = dq[96 * e:96 * e + 96]
+        s1 = jnp.sum(d * wd[1, e, :, c].astype(F32), axis=0, keepdims=True)
+        s2 = jnp.sum(d * wd[2, e, :, c].astype(F32), axis=0, keepdims=True)
+        du, dl = slopes(s1, s2, clip_ref[0, e:e + 1, c], clip_ref[1, e:e + 1, c], most[e:e + 1, c], -most[2 + e:3 + e, c])
+        grad[e:e + 1, c] = du
+        grad[2 + e:3 + e, c] = dl
+    _, me = peer(at, 0)
+    for k in range(WIDE // 256):
+        u = (chunk * 2 * WIDE + core * WIDE) // 256 + k
+        n = lax.rem(u - me + 16, 16)
+        to, _ = peer(at, n)
+
+        @pl.when(n != 0)
+        def _():
+            remote(grad.at[:, unit_cols(u)], inbox.at[n], sems.at[0], sems.at[1], to).start()
 
 
 def slopes(s1, s2, upper, lower, top, low):
@@ -580,15 +588,19 @@
     q.last_mid()
     fp.last_far()
     fp.finish()
+    teacher(xb, 0, raw, w2, hid)
+    q.last_near()
+    teacher(xb, 1, raw, w2, hid)
+    teacher(xb, 2, raw, w2, hid)
+    q.last_far()
     for p in range(3):
-        teacher(xb, p, raw, w2, hid)
-    q.last_near()
-    q.last_far()
+        student_half(xb, p, at["c"], ws, sgu, True)
     q.finish()
+    for p in range(3):
+        student_half(xb, p, 1 - at["c"], ws, sgu, False)
+        student(p, w2, hid, hid_t, sgu)
     gathers_sent(xb, ag_s, ag_r.at[0], moved(at, c=1))
     red = [Reduce(at, k, acc, out, theirs, a_in, b_in, c_in, xb, rs_s, rs_r) for k in range(CHUNKS)]
-    for p in range(3):
-        student(xb, p, ws, w2, hid, hid_t, sgu)
     grad[4:8, :] = jnp.zeros((4, D), F32)
     difference(0, 1 - at["c"], hid_t, wd, down, out)
     red[0].swap()
@@ -596,51 +608,54 @@
     difference(1, 1 - at["c"], hid_t, wd, down, out)
     red[1].swap()
     difference(1, at["c"], hid_t, wd, down, acc)
-    red[0].first()
     difference(2, 1 - at["c"], hid_t, wd, down, out)
     red[2].swap()
     difference(2, at["c"], hid_t, wd, down, acc)
+    red[0].first()
     red[1].first()
+    red[2].first()
     difference(3, 1 - at["c"], hid_t, wd, down, out)
     red[3].swap()
     difference(3, at["c"], hid_t, wd, down, acc)
-    red[2].first()
+    factors(xb, 0, 0, ws, w2, sgu, fac)
+    factors(xb, 0, 1, ws, w2, sgu, fac)
     red[3].first()
-    factors(xb, 0, 0, ws, w2, sgu, fac)
     red[0].first_end()
-    factors(xb, 0, 1, ws, w2, sgu, fac)
+    factors(xb, 1, 0, ws, w2, sgu, fac)
+    factors(xb, 1, 1, ws, w2, sgu, fac)
     red[1].first_end()
+    factors(xb, 2, 0, ws, w2, sgu, fac)
+    red[2].first_end()
+    factors(xb, 2, 1, ws, w2, sgu, fac)
+    red[3].first_end()
     red[0].second_end()
-    factors(xb, 1, 0, ws, w2, sgu, fac)
-    red[2].first_end()
     red[1].second_end()
-    factors(xb, 1, 1, ws, w2, sgu, fac)
-    red[3].first_end()
+    red[2].second_end()
+    red[3].second_end()
     red[0].third_end()
-    red[2].second_end()
-    factors(xb, 2, 0, ws, w2, sgu, fac)
     red[1].third_end()
+    red[2].third_end()
+    red[3].third_end()
     red[0].fourth_end()
-    red[3].second_end()
-    factors(xb, 2, 1, ws, w2, sgu, fac)
-    red[2].third_end()
     red[1].fourth_end()
+    red[2].fourth_end()
+    red[3].fourth_end()
     red[0].fifth_end()
-    red[3].third_end()
-    red[2].fourth_end()
+    back(at, 0, at["c"], xb, hid, wd, dc, fin, dh, grad, d_inbox, d_s, True)
+    red[0].done()
+    back(at, 0, 1 - at["c"], xb, hid, wd, dc, fin, dh, grad, d_inbox, d_s, False)
     red[1].fifth_end()
-    red[0].done()
-    back(0, xb, hid, wd, dc, fin, dh, grad)
-    red[3].fourth_end()
+    back(at, 1, at["c"], xb, hid, wd, dc, fin, dh, grad, d_inbox, d_s, False)
+    red[1].done()
+    back(at, 1, 1 - at["c"], xb, hid, wd, dc, fin, dh, grad, d_inbox, d_s, False)
     red[2].fifth_end()
-    red[1].done()
-    back(1, xb, hid, wd, dc, fin, dh, grad)
+    back(at, 2, at["c"], xb, hid, wd, dc, fin, dh, grad, d_inbox, d_s, False)
+    red[2].done()
+    back(at, 2, 1 - at["c"], xb, hid, wd, dc, fin, dh, grad, d_inbox, d_s, False)
     red[3].fifth_end()
-    red[2].done()
-    back(2, xb, hid, wd, dc, fin, dh, grad)
+    back(at, 3, at["c"], xb, hid, wd, dc, fin, dh, grad, d_inbox, d_s, False)
     red[3].done()
-    back(3, xb, hid, wd, dc, fin, dh, grad)
-    spread_start(at, grad, d_inbox, d_s)
+    back(at, 3, 1 - at["c"], xb, hid, wd, dc, fin, dh, grad, d_inbox, d_s, False)
     row_grads(0, fac, dh, keep, g_out)
     row_grads(1, fac, dh, keep, u_out)
     reduces_sent(xb, rs_s, rs_r, moved(at, c=1))

time: 105 us -> 96.4 us (0.918)
  Pallas kernels: 104 us -> 95.6 us
    pallas_call x1, Pallas kernels: 103 us -> 94.3 us  [on_device(): pl.pallas_call(kernel, out_shape=outs, in_specs=[VM] * 4 + [ANY] * 3 + [V...]
where the time goes in v5:
time: 96.4 us; the launch traced here: 96.2 us
  Pallas kernels  95.6 us (99%)
    pallas_call x1, Pallas kernels, on_device(): pl.pallas_call(kernel, out_shape=outs, in_specs=[VM] * 4 + [ANY] * 3 + [V...  94.3 us

profile of v5, /device:TPU:1, one launch (start us, length us, event | category | flops | bytes accessed | tf_op | source)
XLA Modules:
  0.0 96.2 jit_solution(7416737717857898951)
XLA Ops:
  0.6 94.3 %shard_map.121 = (f32[2,2,96]{2,1,0:T(2,128)}, f32[2,2,96]{2,1,0:T(2,128)}, f32[2,2,256]{2,1,0:T(2,128)}) custom-call(bf16[6,4096]{1,0:T(8,128)(2,1)} %xf_ref.1, bf16[6,4096]{1,0:T(8,128)(2,1)} %xq_ref.1, s32[6,8]{1,0:T(8,128)} %ids_ref.1, f32[6,8]{1,0:T(8,128)} %route_ref.1, bf16[2,96,4096]{2,1,0:T(8,128)(2,1)} %gate_hbm.1, bf16[2,96,4096]{2,1,0:T(8,128)(2,1)} %up_hbm.1, ...), custom_call_target="tpu_custom_call" | custom-call | tf_op jit(solution)/shard_map/pallas_call | solution.py:695
  94.9 1.3 %shard_map.122 = (f32[2,2,96]{2,1,0:T(2,128)}, f32[2,2,96]{2,1,0:T(2,128)}, f32[2,2,256]{2,1,0:T(2,128)}) custom-call(f32[2,2,96]{2,1,0:T(2,128)} %get-tuple-element.6.a, f32[2,2,96]{2,1,0:T(2,128)} %get-tuple-element.7.b, f32[2,2,256]{2,1,0:T(2,128)} %get-tuple-element.8.c), custom_call_target="tpu_custom_call" | custom-call | tf_op jit(solution)/shard_map/pallas_call | solution.py:704

commit v6 on v5

--- a/solution.py
+++ b/solution.py
@@ -11,6 +11,8 @@
 F32 = jnp.float32
 ORDERS = ("xyz", "yzx", "zxy")
 CHUNKS = 4
+TWO_WAY = (False, True, True, False)
+RING_OUT = (True, True, True, True)
 WIDE = 2048 // CHUNKS
 
 
@@ -43,8 +45,11 @@
     return pl.ds(pl.multiple_of(c * 2048 + y * 512, 512), 512)
 
 
-def rows_of(at, done):
-    return [slice(None) if a in done else pl.ds(at[a], 1) for a in "zx"]
+def rows_of(at, done, half=None):
+    rows = [slice(None) if a in done else pl.ds(at[a], 1) for a in "zx"]
+    if half is not None:
+        rows[0 if "z" in done else 1] = pl.ds(2 * half, 2)
+    return rows
 
 
 def ring_pos(at, part, phase, ahead):
@@ -127,9 +132,10 @@
 
 
 class Reduce:
-    def __init__(self, at, chunk, acc, out, theirs, a_in, b_in, c_in, buf, send, recv):
+    def __init__(self, at, chunk, acc, out, theirs, h_in, a_in, b_in, c_in, buf, send, recv):
+        self.two_way, self.ring_out = TWO_WAY[chunk], RING_OUT[chunk]
         self.at, self.chunk, self.acc, self.out, self.theirs = at, chunk, acc, out, theirs
-        self.ins = {2: a_in, 1: b_in, 0: c_in}
+        self.halves, self.ins = h_in, {2: a_in, 1: b_in, 0: c_in}
         self.buf, self.send, self.recv = buf, send, recv
         self.partner = moved(at, c=1)
 
@@ -139,19 +145,20 @@
     def landed(self, ref, recv):
         remote(ref, ref, self.send.at[0], self.recv.at[self.chunk, recv], self.partner).wait_recv()
 
-    def own(self, part, phase, ahead):
+    def own(self, part, phase, ahead, half=None):
         where = ring_pos(self.at, part, phase, ahead)
         done = ORDERS[part][:phase]
-        rows = rows_of(where, done)
+        rows = rows_of(where, done, half)
         width = WIDE if "y" in done else WIDE // 4
         base = 0 if "y" in done else where["y"] * width
         return (self.chunk, part, rows[0], rows[1], slice(None), pl.ds(pl.multiple_of(base, width), width))
 
-    def whole(self, part, phase):
+    def whole(self, part, phase, ahead=0, half=None):
+        where = ring_pos(self.at, part, phase, ahead)
         done = ORDERS[part][:phase]
-        rows = rows_of(self.at, done)
+        rows = rows_of(where, done, half)
         width = WIDE if "y" in done else WIDE // 4
-        base = self.chunk * 2 * WIDE + self.at["c"] * WIDE + (0 if "y" in done else self.at["y"] * width)
+        base = self.chunk * 2 * WIDE + where["c"] * WIDE + (0 if "y" in done else where["y"] * width)
         return (0, part, rows[0], rows[1], slice(None), pl.ds(pl.multiple_of(base, width), width))
 
     def swap(self):
@@ -159,14 +166,9 @@
 
     def total(self, part, phase, arrived):
         sums = self.acc[self.own(part, phase, 0)].astype(F32)
-        for n in range(3):
+        for n in range(2 if arrived == 2 and self.two_way else 3):
             sums = sums + self.ins[arrived][part][self.chunk, n].astype(F32)
         return sums
-
-    def hand_on(self, part, phase):
-        for n in (2, 1, 3):
-            self.push(self.acc.at[self.own(part, phase, n if phase else 0)], self.ins[phase][part].at[self.chunk, n - 1],
-                      1 if phase == 2 else 2, 3 - phase, ring_step(self.at, part, phase, n))
 
     def first(self):
         self.landed(self.theirs.at[self.chunk], 0)
@@ -178,45 +180,79 @@
             return carry
         lax.fori_loop(0, 12, rows, 0)
         for part in range(3):
-            self.hand_on(part, 2)
+            if not self.two_way:
+                for n in (2, 1, 3):
+                    self.push(self.acc.at[self.own(part, 2, n)], self.ins[2][part].at[self.chunk, n - 1], 1, 2,
+                              ring_step(self.at, part, 2, n))
+                continue
+            for side, step in ((0, 1), (1, 3)):
+                self.push(self.acc.at[self.own(part, 2, 2, side)], self.halves[part].at[self.chunk, side], 1, 1,
+                          ring_step(self.at, part, 2, step))
+
+    def first_mid(self):
+        self.landed(self.acc.at[self.chunk, :, 0:1], 1)
+        for part in range(3):
+            for side, step in ((0, 1), (1, 3)):
+                idx = self.own(part, 2, step, side)
+                self.acc[idx] = (self.acc[idx].astype(F32) + self.halves[part][self.chunk, side].astype(F32)).astype(BF)
+                self.push(self.acc.at[self.own(part, 2, step)], self.ins[2][part].at[self.chunk, side], 1, 2,
+                          ring_step(self.at, part, 2, step))
 
     def first_end(self):
-        self.landed(self.acc.at[self.chunk, :, 0:3], 1)
+        self.landed(self.acc.at[self.chunk, :, 0:2 if self.two_way else 3], 2)
         for part in range(3):
             self.acc[self.own(part, 2, 0)] = self.total(part, 2, 2).astype(BF)
-            self.hand_on(part, 1)
+            for n in (2, 1, 3):
+                self.push(self.acc.at[self.own(part, 1, n)], self.ins[1][part].at[self.chunk, n - 1], 2, 3,
+                          ring_step(self.at, part, 1, n))
 
     def second_end(self):
-        self.landed(self.acc.at[self.chunk, :, 0:3, 0:1], 2)
+        self.landed(self.acc.at[self.chunk, :, 0:3, 0:1], 3)
         for part in range(3):
             self.acc[self.own(part, 1, 0)] = self.total(part, 1, 1).astype(BF)
             for n in (2, 1, 3):
-                self.push(self.acc.at[self.own(part, 1, 0)], self.ins[0][part].at[self.chunk, n - 1], 2, 3,
+                self.push(self.acc.at[self.own(part, 1, 0)], self.ins[0][part].at[self.chunk, n - 1], 2, 4,
                           ring_step(self.at, part, 0, n))
 
     def third_end(self):
-        self.landed(self.acc.at[self.chunk, :, 0:3, 0:1], 3)
+        self.landed(self.acc.at[self.chunk, :, 0:3, 0:1], 4)
         for part in range(3):
             block = self.whole(part, 1)
             self.buf[block] = self.total(part, 1, 0).astype(BF)
             for n in (2, 1, 3):
-                self.push(self.buf.at[block], self.buf.at[block], 2, 4, ring_step(self.at, part, 1, n))
+                self.push(self.buf.at[block], self.buf.at[block], 2, 5, ring_step(self.at, part, 1, n))
 
     def fourth_end(self):
-        self.landed(self.acc.at[self.chunk, :, 0:3, 0:1], 4)
-        for n in (2, 1, 3):
-            for part in range(3):
-                block = self.buf.at[self.whole(part, 2)]
-                self.push(block, block, 1, 5, ring_step(self.at, part, 2, n))
+        self.landed(self.acc.at[self.chunk, :, 0:3, 0:1], 5)
+        for part in range(3):
+            block = self.buf.at[self.whole(part, 2)]
+            for step in (1, 3) if self.ring_out else (2, 1, 3):
+                self.push(block, block, 1, 6, ring_step(self.at, part, 2, step))
+
+    def cross(self, aheads):
+        for part in range(3):
+            for ahead in aheads:
+                block = self.buf.at[self.whole(part, 2, ahead)]
+                self.push(block, block, 0, 8, self.partner)
+
+    def fifth_mid(self):
+        self.landed(self.acc.at[self.chunk, :, 0:2], 6)
+        for part in range(3):
+            for side, step in ((0, 1), (1, 3)):
+                block = self.buf.at[self.whole(part, 2, 4 - step, side)]
+                self.push(block, block, 1, 7, ring_step(self.at, part, 2, step))
+        self.cross((0, 1, 3))
 
     def fifth_end(self):
-        self.landed(self.acc.at[self.chunk, :, 0:3], 5)
-        base = self.chunk * 2 * WIDE + self.at["c"] * WIDE
-        block = self.buf.at[0, :, :, :, :, pl.ds(pl.multiple_of(base, WIDE), WIDE)]
-        self.push(block, block, 0, 6, self.partner)
+        if self.ring_out:
+            self.landed(self.acc.at[self.chunk, :, 0:1], 7)
+            self.cross((2,))
+        else:
+            self.landed(self.acc.at[self.chunk, :, 0:3], 6)
+            self.cross((0, 1, 2, 3))
 
     def done(self):
-        self.landed(self.acc.at[self.chunk], 6)
+        self.landed(self.acc.at[self.chunk], 8)
 
 
 def reduces_sent(buf, send, recv, to):
@@ -538,8 +574,8 @@
 def kernel(xf_ref, xq_ref, ids_ref, route_ref, gate_hbm, up_hbm, down_hbm, gc, uc, dc, g_out, u_out, d_out,
            xb, wb, packed, stage, rows_f, spread, raw, down, most, fin, inbox, grad, d_inbox, ws, wd, hid, hid_t, wide, sgu, w2, keep,
            fac, dh, acc, out, theirs, *rest):
-    a_in, b_in, c_in = (rest[3 * k:3 * k + 3] for k in range(3))
-    l_s, t_s, z_s, x_s, m_s, n_s, d_s, ag_s, ag_r, rs_s, rs_r = rest[9:]
+    h_in, a_in, b_in, c_in = (rest[3 * k:3 * k + 3] for k in range(4))
+    l_s, t_s, z_s, x_s, m_s, n_s, d_s, ag_s, ag_r, rs_s, rs_r = rest[12:]
     at = place()
     loads = [pltpu.make_async_copy(down_hbm, down, l_s.at[0])]
     for side, src in enumerate((gate_hbm, up_hbm)):
@@ -600,7 +636,7 @@
         student_half(xb, p, 1 - at["c"], ws, sgu, False)
         student(p, w2, hid, hid_t, sgu)
     gathers_sent(xb, ag_s, ag_r.at[0], moved(at, c=1))
-    red = [Reduce(at, k, acc, out, theirs, a_in, b_in, c_in, xb, rs_s, rs_r) for k in range(CHUNKS)]
+    red = [Reduce(at, k, acc, out, theirs, h_in, a_in, b_in, c_in, xb, rs_s, rs_r) for k in range(CHUNKS)]
     grad[4:8, :] = jnp.zeros((4, D), F32)
     difference(0, 1 - at["c"], hid_t, wd, down, out)
     red[0].swap()
@@ -620,42 +656,48 @@
     factors(xb, 0, 0, ws, w2, sgu, fac)
     factors(xb, 0, 1, ws, w2, sgu, fac)
     red[3].first()
+    factors(xb, 1, 0, ws, w2, sgu, fac)
     red[0].first_end()
-    factors(xb, 1, 0, ws, w2, sgu, fac)
+    red[1].first_mid()
+    red[2].first_mid()
     factors(xb, 1, 1, ws, w2, sgu, fac)
+    factors(xb, 2, 0, ws, w2, sgu, fac)
+    factors(xb, 2, 1, ws, w2, sgu, fac)
+    red[0].second_end()
     red[1].first_end()
-    factors(xb, 2, 0, ws, w2, sgu, fac)
+    red[3].first_end()
     red[2].first_end()
-    factors(xb, 2, 1, ws, w2, sgu, fac)
-    red[3].first_end()
-    red[0].second_end()
+    red[0].third_end()
     red[1].second_end()
+    red[3].second_end()
     red[2].second_end()
-    red[3].second_end()
-    red[0].third_end()
+    red[0].fourth_end()
     red[1].third_end()
+    red[3].third_end()
     red[2].third_end()
-    red[3].third_end()
-    red[0].fourth_end()
+    red[0].fifth_mid()
     red[1].fourth_end()
+    red[3].fourth_end()
     red[2].fourth_end()
-    red[3].fourth_end()
     red[0].fifth_end()
     back(at, 0, at["c"], xb, hid, wd, dc, fin, dh, grad, d_inbox, d_s, True)
+    red[1].fifth_mid()
     red[0].done()
     back(at, 0, 1 - at["c"], xb, hid, wd, dc, fin, dh, grad, d_inbox, d_s, False)
+    red[3].fifth_mid()
+    red[2].fifth_mid()
     red[1].fifth_end()
     back(at, 1, at["c"], xb, hid, wd, dc, fin, dh, grad, d_inbox, d_s, False)
+    red[3].fifth_end()
+    back(at, 3, at["c"], xb, hid, wd, dc, fin, dh, grad, d_inbox, d_s, False)
     red[1].done()
     back(at, 1, 1 - at["c"], xb, hid, wd, dc, fin, dh, grad, d_inbox, d_s, False)
     red[2].fifth_end()
     back(at, 2, at["c"], xb, hid, wd, dc, fin, dh, grad, d_inbox, d_s, False)
+    red[3].done()
+    back(at, 3, 1 - at["c"], xb, hid, wd, dc, fin, dh, grad, d_inbox, d_s, False)
     red[2].done()
     back(at, 2, 1 - at["c"], xb, hid, wd, dc, fin, dh, grad, d_inbox, d_s, False)
-    red[3].fifth_end()
-    back(at, 3, at["c"], xb, hid, wd, dc, fin, dh, grad, d_inbox, d_s, False)
-    red[3].done()
-    back(at, 3, 1 - at["c"], xb, hid, wd, dc, fin, dh, grad, d_inbox, d_s, False)
     row_grads(0, fac, dh, keep, g_out)
     row_grads(1, fac, dh, keep, u_out)
     reduces_sent(xb, rs_s, rs_r, moved(at, c=1))
@@ -690,7 +732,9 @@
                ((384, 768), F32),
                ((192, 768), F32), ((2, 4, 192, 1), F32), ((4, 192, 768), F32), ((192, 768), F32)]
     scratch += [((CHUNKS, 3, 4, 4, 16, WIDE), BF)] * 3
-    scratch += [((CHUNKS, 3) + phase_shape(p, phase), BF) for phase in (2, 1, 1) for p in range(3)]
+    scratch += [((CHUNKS, 2) + shape, BF) for shape in ((1, 2, 16, WIDE), (2, 1, 16, WIDE), (2, 4, 16, WIDE // 4))]
+    scratch += [((CHUNKS, 3) + phase_shape(p, 2), BF) for p in range(3)]
+    scratch += [((CHUNKS, 3) + phase_shape(p, 1), BF) for phase in range(2) for p in range(3)]
     outs = (sds((2, 2, 96), F32), sds((2, 2, 96), F32), sds((2, 2, 256), F32))
     made = pl.pallas_call(
         kernel,
@@ -698,7 +742,7 @@
         in_specs=[VM] * 4 + [ANY] * 3 + [VM] * 3,
         out_specs=(VM,) * 3,
         scratch_shapes=[pltpu.VMEM(s, t) for s, t in scratch] + [SEM((5,))] + [SEM((2,))] * 6 + [
-            SEM((3,)), SEM((2, 6)), SEM((3,)), SEM((CHUNKS, 7))],
+            SEM((3,)), SEM((2, 6)), SEM((3,)), SEM((CHUNKS, 9))],
         compiler_params=pltpu.CompilerParams(collective_id=0, has_side_effects=True, vmem_limit_bytes=62 << 20),
     )(x_fp, x_q, expert_ids, route_weight, gate_weight, up_weight, down_weight, gate_clip, up_clip, down_clip)
     return pl.pallas_call(hand_over, out_shape=outs, in_specs=[VM] * 3, out_specs=(VM,) * 3)(*made)

time: 96.4 us -> 93.5 us (0.970)
  Pallas kernels: 95.6 us -> 92.1 us
    pallas_call x1, Pallas kernels: 94.3 us -> 90.9 us  [on_device(): pl.pallas_call(kernel, out_shape=outs, in_specs=[VM] * 4 + [ANY] * 3 + [V...]
where the time goes in v6:
time: 93.5 us; the launch traced here: 92.8 us
  Pallas kernels  92.1 us (99%)
    pallas_call x1, Pallas kernels, on_device(): pl.pallas_call(kernel, out_shape=outs, in_specs=[VM] * 4 + [ANY] * 3 + [V...  90.9 us

profile of v6, /device:TPU:1, one launch (start us, length us, event | category | flops | bytes accessed | tf_op | source)
XLA Modules:
  0.0 92.8 jit_solution(4491299582324691503)
XLA Ops:
  0.6 90.9 %shard_map.121 = (f32[2,2,96]{2,1,0:T(2,128)}, f32[2,2,96]{2,1,0:T(2,128)}, f32[2,2,256]{2,1,0:T(2,128)}) custom-call(bf16[6,4096]{1,0:T(8,128)(2,1)} %xf_ref.1, bf16[6,4096]{1,0:T(8,128)(2,1)} %xq_ref.1, s32[6,8]{1,0:T(8,128)} %ids_ref.1, f32[6,8]{1,0:T(8,128)} %route_ref.1, bf16[2,96,4096]{2,1,0:T(8,128)(2,1)} %gate_hbm.1, bf16[2,96,4096]{2,1,0:T(8,128)(2,1)} %up_hbm.1, ...), custom_call_target="tpu_custom_call" | custom-call | tf_op jit(solution)/shard_map/pallas_call | solution.py:739
  91.5 1.3 %shard_map.122 = (f32[2,2,96]{2,1,0:T(2,128)}, f32[2,2,96]{2,1,0:T(2,128)}, f32[2,2,256]{2,1,0:T(2,128)}) custom-call(f32[2,2,96]{2,1,0:T(2,128)} %get-tuple-element.6.a, f32[2,2,96]{2,1,0:T(2,128)} %get-tuple-element.7.b, f32[2,2,256]{2,1,0:T(2,128)} %get-tuple-element.8.c), custom_call_target="tpu_custom_call" | custom-call | tf_op jit(solution)/shard_map/pallas_call | solution.py:748

commit v7 on v6

--- a/solution.py
+++ b/solution.py
@@ -627,8 +627,8 @@
     teacher(xb, 0, raw, w2, hid)
     q.last_near()
     teacher(xb, 1, raw, w2, hid)
+    q.last_far()
     teacher(xb, 2, raw, w2, hid)
-    q.last_far()
     for p in range(3):
         student_half(xb, p, at["c"], ws, sgu, True)
     q.finish()

time: 93.5 us -> 93.9 us (level)
  no operation moved by 1% of the time
where the time goes in v7:
time: 93.9 us; the launch traced here: 92.9 us
  Pallas kernels  92.2 us (98%)
    pallas_call x1, Pallas kernels, on_device(): pl.pallas_call(kernel, out_shape=outs, in_specs=[VM] * 4 + [ANY] * 3 + [V...  91 us

profile of v7, /device:TPU:1, one launch (start us, length us, event | category | flops | bytes accessed | tf_op | source)
XLA Modules:
  0.0 92.9 jit_solution(4779161064229608097)
XLA Ops:
  0.6 91.0 %shard_map.121 = (f32[2,2,96]{2,1,0:T(2,128)}, f32[2,2,96]{2,1,0:T(2,128)}, f32[2,2,256]{2,1,0:T(2,128)}) custom-call(bf16[6,4096]{1,0:T(8,128)(2,1)} %xf_ref.1, bf16[6,4096]{1,0:T(8,128)(2,1)} %xq_ref.1, s32[6,8]{1,0:T(8,128)} %ids_ref.1, f32[6,8]{1,0:T(8,128)} %route_ref.1, bf16[2,96,4096]{2,1,0:T(8,128)(2,1)} %gate_hbm.1, bf16[2,96,4096]{2,1,0:T(8,128)(2,1)} %up_hbm.1, ...), custom_call_target="tpu_custom_call" | custom-call | tf_op jit(solution)/shard_map/pallas_call | solution.py:739
  91.6 1.3 %shard_map.122 = (f32[2,2,96]{2,1,0:T(2,128)}, f32[2,2,96]{2,1,0:T(2,128)}, f32[2,2,256]{2,1,0:T(2,128)}) custom-call(f32[2,2,96]{2,1,0:T(2,128)} %get-tuple-element.6.a, f32[2,2,96]{2,1,0:T(2,128)} %get-tuple-element.7.b, f32[2,2,256]{2,1,0:T(2,128)} %get-tuple-element.8.c), custom_call_target="tpu_custom_call" | custom-call | tf_op jit(solution)/shard_map/pallas_call | solution.py:748
